TPU v7x, 256 devices: a whole 4x4x8 slice. The times are simulated.
256 devices in a mesh: dp: 128 (over x, z, y), pair: 2 (over core).
Axes of the slice: x: 4, y: 4, z: 8, core: 2. Of those that a mesh axis runs over, the one named last changes fastest.
Arguments:
- pool: bfloat16 [256, 2, 32768], P(None, None, 'dp'), may hold values from -20 to 20, as said below
- crop_ids: int32 [256, 3], replicated, may hold values from 0 to 255
- crop_corners: int32 [256, 3, 3], replicated, may hold values from 0 to 20
- counts: int32 [256], replicated, may hold values from 1 to 3, 512 in all
- conv_first: float32 [27, 32], replicated, may hold values from -1.25 to 1.25
- conv_second: float32 [27, 32, 32], replicated, may hold values from -0.21875 to 0.21875
- norm_gain: float32 [32], replicated, may hold values from 0.25 to 1.75
- head_weight: float32 [32], replicated, may hold values from -1 to 1
- momentum_first: float32 [27, 32], replicated, may hold values from -0.4375 to 0.4375
- momentum_second: float32 [27, 32, 32], replicated, may hold values from -0.0078125 to 0.0078125
- momentum_gain: float32 [32], replicated, may hold values from -0.4375 to 0.4375
- momentum_head: float32 [32], replicated, may hold values from -0.4375 to 0.4375
- variance_first: float32 [27, 32], replicated, may hold values from 0.0001 to 0.01
- variance_second: float32 [27, 32, 32], replicated, may hold values from 0.0001 to 0.01
- variance_gain: float32 [32], replicated, may hold values from 0.0001 to 0.01
- variance_head: float32 [32], replicated, may hold values from 0.0001 to 0.01
Outputs:
- update_first: float32 [27, 32], replicated
- update_second: float32 [27, 32, 32], replicated
- update_gain: float32 [32], replicated
- update_head: float32 [32], replicated
- next_momentum_first: float32 [27, 32], replicated
- next_momentum_second: float32 [27, 32, 32], replicated
- next_momentum_gain: float32 [32], replicated
- next_momentum_head: float32 [32], replicated
Inputs may be any that keep to these rules, and one draw needn't show every extreme that they name: `pool`: channel 0 holds intensities, channel 1 boundary targets within 0 to 1. The counts sum to exactly 512, and some row requests 3 crops.
All inputs are finite; a program needn't handle non-finite values.
Results may differ from a plain program's by a relative error of at most 0.0041.
Values may be sent and summed in bfloat16 or wider, within the bound.
A program may use at most 64 MiB of HBM per device.

v0:
```python
import functools

import jax
import jax.numpy as jnp
from jax import lax
from jax.experimental import pallas as pl
from jax.experimental.pallas import tpu as pltpu
from jax.sharding import PartitionSpec as P

CH = 32
CROP = 12
BLOCK = 32


SIDE = 16
PLANE = SIDE * SIDE
LANES = 2 * PLANE
VOXELS = CROP * CROP * CROP
BAND = 6 * CH


def iota(shape, axis):
    return lax.broadcasted_iota(jnp.int32, shape, axis)


def nt(a, b):
    return lax.dot_general(a, b, (((1,), (1,)), ((), ())), preferred_element_type=jnp.float32)


def nn(a, b):
    return jnp.dot(a, b, preferred_element_type=jnp.float32)


def onehot(condition):
    return jnp.where(condition, 1.0, 0.0).astype(jnp.bfloat16)


def valid_lanes(rows):
    lane = iota((rows, PLANE), 1)
    return (lane % SIDE < CROP) & ((lane // SIDE) % SIDE < CROP)


def shifted(value, offset):
    amount = (-offset) % PLANE
    return pltpu.roll(value, amount, 1) if amount else value


def halves(ref, rows, crop):
    return ref[rows, crop * PLANE : (crop + 1) * PLANE]


def expand_first(conv_first, toeplitz_first):
    weights = conv_first[...].astype(jnp.bfloat16)
    repeat = onehot(iota((12 * CH, CH), 0) % CH == iota((12 * CH, CH), 1))
    row, column = iota((12 * CH, 144), 0), iota((12 * CH, 144), 1)
    place = row // CH
    step = column % 16 - (2 * (place % 6) + place // 6) + 1
    total = jnp.zeros((12 * CH, 144), jnp.float32)
    for dx in range(3):
        tap = onehot(iota((144, 27), 0) // 16 + 9 * dx == iota((144, 27), 1))
        spread = nn(tap, weights).astype(jnp.bfloat16)
        total = jnp.where(step == dx, nt(repeat, spread), total)
    toeplitz_first[...] = total.astype(jnp.bfloat16)


def expand_second(conv_second, forward, backward):
    eye = onehot(iota((CH, CH), 0) == iota((CH, CH), 1))
    for tap in range(9):
        blocks = [conv_second[9 * dx + tap] for dx in range(3)]
        zero = jnp.zeros((CH, 256 - 3 * CH), jnp.float32)
        group = slice(tap * 256, tap * 256 + 256)
        strip = jnp.concatenate([blocks[2], blocks[1], blocks[0], zero], axis=1)
        stacked = jnp.concatenate(blocks, axis=0).astype(jnp.bfloat16)
        turned = jnp.concatenate([nt(eye, stacked), zero], axis=1)
        for i in range(6):
            rows = slice(i * CH, i * CH + CH)
            amount = (CH * (i - 1)) % 256
            moved = pltpu.roll(strip, amount, 1) if amount else strip
            backward[rows, group] = moved.astype(jnp.bfloat16)
            moved = pltpu.roll(turned, amount, 1) if amount else turned
            forward[rows, group] = moved.astype(jnp.bfloat16)


def clear_ends(stack):
    for parity in range(2):
        for tap in range(9):
            stack[parity, tap * 256 + BAND : tap * 256 + 256, :] = jnp.zeros((256 - BAND, LANES), jnp.bfloat16)


def crop_gradients(
    x, t, gain_ref, head_ref, packed,
    toeplitz_first, forward, backward, patches, hidden, hidden_stack, second, logits, cotangent, cotangent_stack,
):
    valid = valid_lanes(1)
    for crop in range(2):
        half = slice(crop * PLANE, (crop + 1) * PLANE)
        source = x[:, half].astype(jnp.float32)
        for tap in range(9):
            offset = SIDE * (tap // 3 - 1) + tap % 3 - 1
            patches[tap * 16 : tap * 16 + 16, half] = shifted(source, offset).astype(jnp.bfloat16)
    for crop in range(2):
        half = slice(crop * PLANE, (crop + 1) * PLANE)
        for parity in range(2):
            rows = slice(parity * BAND, parity * BAND + BAND)
            first_map = nn(toeplitz_first[rows, :], patches[:, half])
            value = jnp.where(valid, jnp.maximum(first_map, 0.0), 0.0)
            hidden[rows, half] = value.astype(jnp.bfloat16)
            for tap in range(9):
                offset = 2 * (SIDE * (tap // 3 - 1) + tap % 3 - 1)
                hidden_stack[parity, tap * 256 : tap * 256 + BAND, half] = shifted(value, offset).astype(jnp.bfloat16)
    for parity in range(2):
        second[parity * BAND : parity * BAND + BAND, :] = nn(forward[...], hidden_stack[parity])
    gain = gain_ref[...]
    head = head_ref[...]
    scale = 1.0 / VOXELS
    columns = []
    for crop in range(2):
        half = slice(crop * PLANE, (crop + 1) * PLANE)
        total = jnp.zeros((CH, PLANE), jnp.float32)
        for m in range(12):
            total = total + second[m * CH : m * CH + CH, half]
        center = jnp.sum(jnp.where(valid, total, 0.0), axis=1, keepdims=True) * scale
        total = jnp.zeros((CH, PLANE), jnp.float32)
        for m in range(12):
            away = second[m * CH : m * CH + CH, half] - center
            total = total + away * away
        spread = jnp.sum(jnp.where(valid, total, 0.0), axis=1, keepdims=True) * scale
        inverse = lax.rsqrt(spread + 1e-05)
        columns.append(inverse)
        for m in range(12):
            rows = slice(m * CH, m * CH + CH)
            hat = (second[rows, half] - center) * inverse
            second[rows, half] = hat
            joined = (jnp.maximum(hat * gain, 0.0) + hidden[rows, half].astype(jnp.float32)).astype(jnp.bfloat16)
            logits[m : m + 1, half] = jnp.sum(joined.astype(jnp.float32) * head, axis=0, keepdims=True)
    slope = 1.0 / (1.0 + jnp.exp(-logits[0:12, :])) - t[...]
    both = jnp.concatenate([valid, valid], axis=1)
    logits[0:12, :] = jnp.where(both, slope * scale, 0.0)
    grad_gain = jnp.zeros((CH, 1), jnp.float32)
    grad_head = jnp.zeros((CH, 1), jnp.float32)
    for crop in range(2):
        half = slice(crop * PLANE, (crop + 1) * PLANE)
        sum_plain = jnp.zeros((CH, PLANE), jnp.float32)
        sum_hat = jnp.zeros((CH, PLANE), jnp.float32)
        sum_head = jnp.zeros((CH, PLANE), jnp.float32)
        for m in range(12):
            rows = slice(m * CH, m * CH + CH)
            hat = second[rows, half]
            normed = hat * gain
            slope = logits[m : m + 1, half]
            joined = (jnp.maximum(normed, 0.0) + hidden[rows, half].astype(jnp.float32)).astype(jnp.bfloat16)
            sum_head = sum_head + joined.astype(jnp.float32) * slope
            passed = jnp.where(normed > 0.0, slope, 0.0)
            sum_plain = sum_plain + passed
            sum_hat = sum_hat + passed * hat
        grad_head = grad_head + jnp.sum(sum_head, axis=1, keepdims=True)
        mean_plain = head * jnp.sum(sum_plain, axis=1, keepdims=True)
        mean_hat = head * jnp.sum(sum_hat, axis=1, keepdims=True)
        grad_gain = grad_gain + mean_hat
        mean_plain = mean_plain * scale
        mean_hat = mean_hat * scale
        factor = columns[crop] * gain
        for parity in range(2):
            for i in range(6):
                m = parity * 6 + i
                rows = slice(m * CH, m * CH + CH)
                hat = second[rows, half]
                slope = logits[m : m + 1, half]
                passed = jnp.where(hat * gain > 0.0, head * slope, 0.0)
                value = jnp.where(valid, factor * (passed - mean_plain - hat * mean_hat), 0.0)
                cotangent[parity, i * CH : i * CH + CH, half] = value.astype(jnp.bfloat16)
                for tap in range(9):
                    offset = -2 * (SIDE * (tap // 3 - 1) + tap % 3 - 1)
                    place = tap * 256 + i * CH
                    cotangent_stack[parity, place : place + CH, half] = shifted(value, offset).astype(jnp.bfloat16)
    for parity in range(2):
        cotangent[parity, BAND:256, :] = jnp.zeros((256 - BAND, LANES), jnp.bfloat16)
    lane = iota((CH, 128), 1)
    for tap in range(9):
        group = slice(tap * 256, tap * 256 + BAND)
        products = nt(hidden_stack[0, group, :], cotangent[0]) + nt(hidden_stack[1, group, :], cotangent[1])
        total = jnp.zeros((CH, 256), jnp.float32)
        for i in range(6):
            band = products[i * CH : i * CH + CH, :]
            amount = (-CH * (i - 1)) % 256
            total = total + (pltpu.roll(band, amount, 1) if amount else band)
        total = total[:, 0:128]
        at = tap * CH
        if at < 216:
            count = min(CH, 216 - at)
            packed[at : at + count, :] = jnp.where(lane < 96, total, 0.0)[0:count]
        if at + CH > 216:
            skip = max(0, 216 - at)
            for j in range(3):
                moved = pltpu.roll(total, 96 - CH * j, 1)
                moved = jnp.where(lane >= 96, moved, 0.0)[skip:CH]
                to = 72 * j + at + skip - 216
                packed[to : to + CH - skip, :] = packed[to : to + CH - skip, :] + moved
    for parity in range(2):
        rows = slice(parity * BAND, parity * BAND + BAND)
        for crop in range(2):
            half = slice(crop * PLANE, (crop + 1) * PLANE)
            back = nn(backward[...], cotangent_stack[parity, :, half])
            for i in range(6):
                m = parity * 6 + i
                at = slice(m * CH, m * CH + CH)
                whole = back[i * CH : i * CH + CH, :] + head * logits[m : m + 1, half]
                alive = hidden[at, half].astype(jnp.float32) > 0.0
                second[at, half] = jnp.where(alive, whole, 0.0)
    products = nt(patches[...], second[...].astype(jnp.bfloat16))
    row, column = iota((144, 12 * CH), 0), iota((144, 12 * CH), 1)
    place = column // CH
    step = row % 16 - (2 * (place % 6) + place // 6) + 1
    lane = iota((9, 128), 1)
    small = jnp.zeros((9, 128), jnp.float32)
    for dx in range(3):
        part = jnp.where(step == dx, products, 0.0)
        part = jnp.sum(part.reshape(9, 16, 12 * CH), axis=1)
        part = part[:, 0:128] + part[:, 128:256] + part[:, 256:384]
        part = part + pltpu.roll(part, 64, 1)
        part = part + pltpu.roll(part, 32, 1)
        small = jnp.where(lane // CH == dx, part, small)
    packed[216:225, :] = small
    pick = iota((CH, 128), 0) + 96 == iota((CH, 128), 1)
    packed[216:217, :] = packed[216:217, :] + jnp.sum(jnp.where(pick, grad_gain, 0.0), axis=0, keepdims=True)
    packed[217:218, :] = packed[217:218, :] + jnp.sum(jnp.where(pick, grad_head, 0.0), axis=0, keepdims=True)
    packed[225:256, :] = jnp.zeros((31, 128), jnp.float32)


def gradient_kernel(
    x, t, conv_first, conv_second, gain, head, packed,
    toeplitz_first, forward, backward, patches, hidden, hidden_stack, second, logits, cotangent, cotangent_stack,
):
    expand_first(conv_first, toeplitz_first)
    expand_second(conv_second, forward, backward)
    clear_ends(hidden_stack)
    clear_ends(cotangent_stack)
    crop_gradients(
        x, t, gain, head, packed,
        toeplitz_first, forward, backward, patches, hidden, hidden_stack, second, logits, cotangent, cotangent_stack,
    )


COMPUTE_SCRATCH = [
    pltpu.VMEM((12 * CH, 144), jnp.bfloat16),
    pltpu.VMEM((BAND, 9 * 256), jnp.bfloat16),
    pltpu.VMEM((BAND, 9 * 256), jnp.bfloat16),
    pltpu.VMEM((144, LANES), jnp.bfloat16),
    pltpu.VMEM((12 * CH, LANES), jnp.bfloat16),
    pltpu.VMEM((2, 9 * 256, LANES), jnp.bfloat16),
    pltpu.VMEM((12 * CH, LANES), jnp.float32),
    pltpu.VMEM((16, LANES), jnp.float32),
    pltpu.VMEM((2, 256, LANES), jnp.bfloat16),
    pltpu.VMEM((2, 9 * 256, LANES), jnp.bfloat16),
]


def gradients(x, t, conv_first, conv_second, norm_gain, head_weight):
    head = head_weight.astype(jnp.bfloat16).astype(jnp.float32)
    return pl.pallas_call(
        gradient_kernel,
        out_shape=jax.ShapeDtypeStruct((256, 128), jnp.float32),
        in_specs=[pl.BlockSpec(memory_space=pltpu.VMEM)] * 6,
        out_specs=pl.BlockSpec(memory_space=pltpu.VMEM),
        scratch_shapes=COMPUTE_SCRATCH,
        compiler_params=pltpu.CompilerParams(vmem_limit_bytes=40 * 1024 * 1024),
    )(x, t, conv_first, conv_second, norm_gain.reshape(CH, 1), head.reshape(CH, 1))


def unpack(total):
    second = []
    for dx in range(3):
        j = 2 - dx
        second.append(total[0:216, CH * j : CH * j + CH])
        second.append(total[72 * j : 72 * j + 72, 96:128])
    second = jnp.concatenate(second, axis=0).reshape(27, CH, CH)
    first = jnp.concatenate([total[216:225, CH * dx : CH * dx + CH] for dx in range(3)], axis=0)
    return first, second, total[216, 96:128], total[217, 96:128]


MESH = pl.DeviceIdType.MESH
ROWS = 16


def plane_peer(k):
    dp = lax.axis_index("dp")
    x = lax.rem(dp // 32 + k // 4, 4)
    y = lax.rem(lax.rem(dp, 4) + k % 4, 4)
    z = lax.rem(dp // 4, 8)
    return (x * 32 + z * 4 + y, lax.axis_index("pair")), x * 4 + y


def column_peer(k):
    dp = lax.axis_index("dp")
    z = lax.rem(lax.rem(dp // 4, 8) + k // 2, 8)
    core = lax.rem(lax.axis_index("pair") + k % 2, 2)
    return ((dp // 32) * 32 + z * 4 + lax.rem(dp, 4), core), z * 2 + core


def sum_kernel(part, out, first, second, send, recv):
    barrier = pltpu.get_barrier_semaphore()
    for k in range(1, 16):
        pl.semaphore_signal(barrier, inc=1, device_id=plane_peer(k)[0], device_id_type=MESH)
        pl.semaphore_signal(barrier, inc=1, device_id=column_peer(k)[0], device_id_type=MESH)
    pl.semaphore_wait(barrier, 30)
    _, plane_me = plane_peer(0)
    _, column_me = column_peer(0)

    def rows(place):
        return pl.ds(pl.multiple_of(place * ROWS, ROWS), ROWS)

    def exchange(stage, peer, source, target):
        copies = []
        for k in range(1, 16):
            device, place = peer(k)
            copy = pltpu.make_async_remote_copy(
                src_ref=source(place), dst_ref=target,
                send_sem=send.at[stage, k], recv_sem=recv.at[stage, k],
                device_id=device, device_id_type=MESH,
            )
            copy.start()
            copies.append(copy)
        return copies

    copies = exchange(0, plane_peer, lambda place: part.at[rows(place)], first.at[plane_me])
    first[plane_me] = part[rows(plane_me)]
    for copy in copies:
        copy.wait()
    total = first[0]
    for k in range(1, 16):
        total = total + first[k]
    second[column_me] = total
    copies = exchange(1, column_peer, lambda place: second.at[column_me], second.at[column_me])
    for copy in copies:
        copy.wait()
    total = second[0]
    for k in range(1, 16):
        total = total + second[k]
    out[rows(plane_me)] = total
    copies = exchange(2, plane_peer, lambda place: out.at[rows(plane_me)], out.at[rows(plane_me)])
    for copy in copies:
        copy.wait()


def sum_everywhere(packed):
    return pl.pallas_call(
        sum_kernel,
        out_shape=jax.ShapeDtypeStruct((16 * ROWS, 128), jnp.float32),
        in_specs=[pl.BlockSpec(memory_space=pltpu.VMEM)],
        out_specs=pl.BlockSpec(memory_space=pltpu.VMEM),
        scratch_shapes=[
            pltpu.VMEM((16, ROWS, 128), jnp.float32),
            pltpu.VMEM((16, ROWS, 128), jnp.float32),
            pltpu.SemaphoreType.DMA((3, 16)),
            pltpu.SemaphoreType.DMA((3, 16)),
        ],
        compiler_params=pltpu.CompilerParams(collective_id=0, has_side_effects=True),
    )(packed)


beta_first = 0.9
beta_second = 0.999


def adam_update(gradient, momentum, variance):
    next_momentum = beta_first * momentum + (1.0 - beta_first) * gradient
    next_variance = beta_second * variance + (1.0 - beta_second) * gradient * gradient
    return next_momentum / (jnp.sqrt(next_variance) + 1e-08), next_momentum


def adam_kernel(inverse_batch, total, *refs):
    moments, variances, updates, nexts = refs[0:4], refs[4:8], refs[8:12], refs[12:16]
    gradient = total[...] * inverse_batch
    for dx in range(3):
        j = 2 - dx
        part = jnp.concatenate(
            [gradient[0:216, CH * j : CH * j + CH], gradient[72 * j : 72 * j + 72, 96:128]], axis=0
        ).reshape(9, CH, CH)
        taps = slice(9 * dx, 9 * dx + 9)
        updates[1][taps], nexts[1][taps] = adam_update(part, moments[1][taps], variances[1][taps])
        part = gradient[216:225, CH * dx : CH * dx + CH]
        updates[0][taps], nexts[0][taps] = adam_update(part, moments[0][taps], variances[0][taps])
    for place in (2, 3):
        part = gradient[214 + place : 215 + place, 96:128]
        updates[place][...], nexts[place][...] = adam_update(part, moments[place][...], variances[place][...])


def adam(total, batch_size, moments, variances):
    rows = [value.reshape(1, CH) if value.ndim == 1 else value for value in (*moments, *variances)]
    shapes = [jax.ShapeDtypeStruct(value.shape, jnp.float32) for value in rows[0:4]]
    results = pl.pallas_call(
        functools.partial(adam_kernel, 1.0 / batch_size),
        out_shape=shapes + shapes,
        in_specs=[pl.BlockSpec(memory_space=pltpu.VMEM)] * 9,
        out_specs=[pl.BlockSpec(memory_space=pltpu.VMEM)] * 8,
    )(total, *rows)
    return tuple(value.reshape(CH) if value.shape == (1, CH) else value for value in results)


SHARE = 2


def crop_order(counts, position):
    starts = jnp.cumsum(counts, dtype=jnp.int32) - counts
    rows = jnp.sum((starts[None, :] <= position[:, None]).astype(jnp.int32), axis=1, dtype=jnp.int32) - 1
    return rows, position - starts[rows]


def shards(
    pool, crop_ids, crop_corners, counts, conv_first, conv_second, norm_gain, head_weight,
    momentum_first, momentum_second, momentum_gain, momentum_head,
    variance_first, variance_second, variance_gain, variance_head,
):
    dp_count = lax.axis_size("dp")
    pair_index = lax.axis_index("pair")
    batch_size = counts.shape[0] * SHARE
    position = pair_index * dp_count * SHARE + jnp.arange(dp_count * SHARE, dtype=jnp.int32)
    rows, slots = crop_order(counts, position)
    wanted = crop_ids[rows, slots].reshape(dp_count, SHARE)
    arrived = lax.all_to_all(pool[wanted], "dp", split_axis=0, concat_axis=3, tiled=True)[0]
    volumes = arrived.reshape(SHARE, 2, BLOCK, BLOCK, BLOCK)
    mine = lax.dynamic_slice_in_dim(rows, lax.axis_index("dp") * SHARE, SHARE)
    mine_slots = lax.dynamic_slice_in_dim(slots, lax.axis_index("dp") * SHARE, SHARE)
    corners = crop_corners[mine, mine_slots]
    windows = [
        lax.dynamic_slice(volumes[s], (0, corners[s, 0], corners[s, 1], corners[s, 2]), (2, CROP, CROP, CROP))
        for s in range(SHARE)
    ]
    windows = jnp.pad(jnp.stack(windows), ((0, 0), (0, 0), (0, 4), (0, 4), (0, 4)))
    windows = windows.transpose(1, 2, 0, 3, 4).reshape(2, SIDE, LANES)
    targets = jnp.concatenate([windows[1, 0:12:2], windows[1, 1:12:2]]).astype(jnp.float32)
    packed = gradients(windows[0], targets, conv_first, conv_second, norm_gain, head_weight)
    total = sum_everywhere(packed)
    return adam(
        total, batch_size,
        (momentum_first, momentum_second, momentum_gain, momentum_head),
        (variance_first, variance_second, variance_gain, variance_head),
    )


def solution(mesh):
    in_specs = (P(None, None, "dp"),) + (P(),) * 15
    return jax.shard_map(shards, mesh=mesh, in_specs=in_specs, out_specs=(P(),) * 8, check_vma=False)
```

profile of v0, /device:TPU:1, one launch (start us, length us, event | category | flops | bytes accessed | tf_op | source)
XLA Modules:
  0.0 78.7 jit_solution(17059589970589518002)
XLA Ops:
  0.6 0.0 copy-start
  0.7 0.0 copy-start.6
  0.7 0.7 copy-done.6
  1.4 0.3 reduce-window.9
  1.7 0.1 slice.43
  1.8 0.1 slice_reduce_fusion
  1.9 0.1 bitcast_subtract_fusion
  2.0 0.2 convert_reduce_fusion
  2.2 1.9 %gather_fusion = s32[256]{0:T(256)S(1)} fusion(s32[256]{0:T(256)S(1)} %get-tuple-element.34, s32[1024]{0:T(1024)S(1)} %pad_clamp_fusion.1), kind=kCustom, calls=%fused_computation | custom fusion | bytes 3072 | tf_op jit(solution)/shard_map/gather | solution.py:406
  4.2 0.0 copy-start.4
  4.2 0.7 copy-done.4
  4.8 2.5 %gather_fusion.1 = s32[256]{0:T(256)S(1)} fusion(s32[256,3]{0,1:T(4,128)S(1)} %copy-done.4, s32[256]{0:T(256)S(1)} %bitcast.48), kind=kCustom, calls=%fused_computation.1 | custom fusion | bytes 4096 | tf_op jit(solution)/shard_map/gather | solution.py:419
  7.3 0.1 reshape.151
  7.5 0.1 reshape.182
  7.6 0.0 copy-done
  7.6 1.9 %gather_fusion.2 = bf16[256,2,256]{2,1,0:T(2,128)(2,1)} fusion(bf16[256,2,256]{2,1,0:T(2,128)(2,1)S(1)} %copy-done, s32[1024]{0:T(1024)S(1)} %pad_clamp_fusion), kind=kCustom, calls=%fused_computation.2 | custom fusion | bytes 525312 | tf_op jit(solution)/shard_map/gather | solution.py:420
  9.6 16.5 %all-to-all-start = ((bf16[128,2,2,256]{3,2,1,0:T(2,128)(2,1)}), bf16[128,2,2,256]{3,2,1,0:T(2,128)(2,1)S(1)}, u32[]{:S(2)}, u32[]{:S(2)}) async-start(bf16[128,2,2,256]{3,2,1,0:T(2,128)(2,1)} %bitcast.7), calls=%async_computation | async-start | bytes 524288 | tf_op jit(solution)/shard_map/all_to_all | solution.py:420
  26.1 0.0 copy-start.5
  26.1 0.7 copy-done.5
  26.8 0.2 copy.37
  27.0 0.1 fusion.15
  27.1 0.6 gather_fusion.3
  27.6 0.6 fusion.20
  35.4 0.0 copy-start.8
  36.0 0.0 copy-done.8
  36.1 0.1 copy.40.head
  36.1 0.0 copy-start.7
  36.2 0.7 copy-done.7
  36.8 0.1 copy.39.gain
  40.8 0.0 all-to-all-done
  40.8 0.2 fusion.19
  41.0 0.2 squeeze.33
  41.3 0.2 squeeze.37
  41.5 0.1 dynamic-slice_bitcast_fusion.1
  41.6 0.1 dynamic-slice_bitcast_fusion
  41.8 0.1 fusion.8
  41.9 0.0 copy-start.2
  41.9 0.3 reshape.152
  42.2 0.2 squeeze.41.x
  42.4 0.0 copy-start.3
  42.5 0.4 copy-done.2
  42.9 0.3 copy-done.3
  43.2 6.2 %shard_map.215.part = f32[256,128]{1,0:T(8,128)S(1)} custom-call(bf16[16,512]{1,0:T(8,128)(2,1)S(1)} %squeeze.41.x, f32[12,512]{1,0:T(8,128)S(1)} %maximum_convert_fusion.t, f32[27,32]{1,0:T(8,128)S(1)} %copy-done.3, f32[27,32,32]{2,1,0:T(8,128)S(1)} %copy-done.2, f32[32,1]{1,0:T(8,128)S(1)} %copy.39.gain, f32[32,1]{1,0:T(8,128)S(1)} %copy.40.head), custom_call_target="tpu_custom_call" | custom-call | tf_op jit(solution)/shard_map/pallas_call | solution.py:260
  49.3 0.0 copy-start.1
  49.4 0.6 copy-done.1
  50.0 26.1 %shard_map.216.total = f32[256,128]{1,0:T(8,128)} custom-call(f32[256,128]{1,0:T(8,128)} %copy-done.1), custom_call_target="tpu_custom_call" | custom-call | tf_op jit(solution)/shard_map/pallas_call | solution.py:346
  76.1 2.5 %shard_map.217 = (f32[27,32]{1,0:T(8,128)}, f32[27,32,32]{2,1,0:T(8,128)}, f32[1,32]{1,0:T(1,128)}, f32[1,32]{1,0:T(1,128)}, f32[27,32]{1,0:T(8,128)}, /*index=5...) custom-call(f32[256,128]{1,0:T(8,128)} %shard_map.216.total, f32[27,32]{1,0:T(8,128)} %refs_0_.1, ...), custom_call_target="tpu_custom_call" | custom-call | tf_op jit(solution)/shard_map/pallas_call | solution.py:391
  (15 shorter events, 0.2 us)
Async XLA Ops:
  0.6 7.0 %copy-start = (bf16[256,2,256]{2,1,0:T(2,128)(2,1)S(1)}, bf16[256,2,256]{2,1,0:T(2,128)(2,1)}, u32[]{:S(2)}) copy-start(bf16[256,2,256]{2,1,0:T(2,128)(2,1)} %param.16) | copy-start | bytes 786436
  0.7 0.7 copy-start.6
  4.2 0.7 copy-start.4
  9.6 31.2 %all-to-all-start = ((bf16[128,2,2,256]{3,2,1,0:T(2,128)(2,1)}), bf16[128,2,2,256]{3,2,1,0:T(2,128)(2,1)S(1)}, u32[]{:S(2)}, u32[]{:S(2)}) async-start(bf16[128,2,2,256]{3,2,1,0:T(2,128)(2,1)} %bitcast.7), calls=%async_computation | async-start | bytes 524288 | tf_op jit(solution)/shard_map/all_to_all | solution.py:420
  26.1 0.7 copy-start.5
  35.4 0.7 copy-start.8
  36.1 0.7 copy-start.7
  41.9 1.0 %copy-start.2 = (f32[27,32,32]{2,1,0:T(8,128)S(1)}, f32[27,32,32]{2,1,0:T(8,128)}, u32[]{:S(2)}) copy-start(f32[27,32,32]{2,1,0:T(8,128)} %conv_second.1) | copy-start | bytes 331780
  42.4 0.8 copy-start.3
  49.3 0.7 copy-start.1
where the time goes:
time: 79.3 us; the launch traced here: 78.7 us
  Pallas kernels  34.7 us (44%)
  starting transfers between devices  16.5 us (21%)
  local copies, waits for them, and re-layouts  13.9 us (18%)
  between operations  12.7 us (16%)
  other arithmetic  0.84 us (1%)
    pallas_call x1, Pallas kernels, sum_everywhere(): pl.pallas_call(sum_kernel, out_shape=jax.ShapeDtypeStruct((16 * ROWS, 128...  26.1 us
    all_to_all x1, starting transfers between devices, shards(): lax.all_to_all(pool[wanted], 'dp', split_axis=0, concat_axis=3, tiled=True)  16.5 us
    pallas_call x1, Pallas kernels, gradients(): pl.pallas_call(gradient_kernel, out_shape=jax.ShapeDtypeStruct((256, 128)...  6.17 us
    unnamed x19, local copies, waits for them, and re-layouts  4.3 us
    pallas_call x1, Pallas kernels, adam(): pl.pallas_call(functools.partial(adam_kernel, 1.0 / batch_size), out_shap...  2.47 us
    gather x1, local copies, waits for them, and re-layouts, shards(): wanted = crop_ids[rows, slots].reshape(dp_count, SHARE)  2.47 us
    gather x1, local copies, waits for them, and re-layouts, crop_order(): return (rows, position - starts[rows])  1.94 us
    gather x1, local copies, waits for them, and re-layouts, shards(): pool[wanted]  1.92 us
  transfers between devices with their start and end apart: 1, of which 0 were waited for; matrix products, arithmetic and copies ran while one was open for 2% of the time, Pallas kernels for 0%

commit v1 on v0

--- a/solution.py
+++ b/solution.py
@@ -10,6 +10,7 @@
 CH = 32
 CROP = 12
 BLOCK = 32
+MOST = 3
 
 
 SIDE = 16
@@ -33,6 +34,10 @@
 
 def onehot(condition):
     return jnp.where(condition, 1.0, 0.0).astype(jnp.bfloat16)
+
+
+def plane_of(m):
+    return 2 * (m % 6) + m // 6
 
 
 def valid_lanes(rows):
@@ -88,13 +93,13 @@
 
 
 def crop_gradients(
-    x, t, gain_ref, head_ref, packed,
+    x, t, gain, head, packed,
     toeplitz_first, forward, backward, patches, hidden, hidden_stack, second, logits, cotangent, cotangent_stack,
 ):
     valid = valid_lanes(1)
     for crop in range(2):
         half = slice(crop * PLANE, (crop + 1) * PLANE)
-        source = x[:, half].astype(jnp.float32)
+        source = x[crop]
         for tap in range(9):
             offset = SIDE * (tap // 3 - 1) + tap % 3 - 1
             patches[tap * 16 : tap * 16 + 16, half] = shifted(source, offset).astype(jnp.bfloat16)
@@ -110,8 +115,6 @@
                 hidden_stack[parity, tap * 256 : tap * 256 + BAND, half] = shifted(value, offset).astype(jnp.bfloat16)
     for parity in range(2):
         second[parity * BAND : parity * BAND + BAND, :] = nn(forward[...], hidden_stack[parity])
-    gain = gain_ref[...]
-    head = head_ref[...]
     scale = 1.0 / VOXELS
     columns = []
     for crop in range(2):
@@ -132,8 +135,8 @@
             hat = (second[rows, half] - center) * inverse
             second[rows, half] = hat
             joined = (jnp.maximum(hat * gain, 0.0) + hidden[rows, half].astype(jnp.float32)).astype(jnp.bfloat16)
-            logits[m : m + 1, half] = jnp.sum(joined.astype(jnp.float32) * head, axis=0, keepdims=True)
-    slope = 1.0 / (1.0 + jnp.exp(-logits[0:12, :])) - t[...]
+            logits[plane_of(m) : plane_of(m) + 1, half] = jnp.sum(joined.astype(jnp.float32) * head, axis=0, keepdims=True)
+    slope = 1.0 / (1.0 + jnp.exp(-logits[0:12, :])) - t
     both = jnp.concatenate([valid, valid], axis=1)
     logits[0:12, :] = jnp.where(both, slope * scale, 0.0)
     grad_gain = jnp.zeros((CH, 1), jnp.float32)
@@ -147,7 +150,7 @@
             rows = slice(m * CH, m * CH + CH)
             hat = second[rows, half]
             normed = hat * gain
-            slope = logits[m : m + 1, half]
+            slope = logits[plane_of(m) : plane_of(m) + 1, half]
             joined = (jnp.maximum(normed, 0.0) + hidden[rows, half].astype(jnp.float32)).astype(jnp.bfloat16)
             sum_head = sum_head + joined.astype(jnp.float32) * slope
             passed = jnp.where(normed > 0.0, slope, 0.0)
@@ -165,7 +168,7 @@
                 m = parity * 6 + i
                 rows = slice(m * CH, m * CH + CH)
                 hat = second[rows, half]
-                slope = logits[m : m + 1, half]
+                slope = logits[plane_of(m) : plane_of(m) + 1, half]
                 passed = jnp.where(hat * gain > 0.0, head * slope, 0.0)
                 value = jnp.where(valid, factor * (passed - mean_plain - hat * mean_hat), 0.0)
                 cotangent[parity, i * CH : i * CH + CH, half] = value.astype(jnp.bfloat16)
@@ -204,7 +207,7 @@
             for i in range(6):
                 m = parity * 6 + i
                 at = slice(m * CH, m * CH + CH)
-                whole = back[i * CH : i * CH + CH, :] + head * logits[m : m + 1, half]
+                whole = back[i * CH : i * CH + CH, :] + head * logits[plane_of(m) : plane_of(m) + 1, half]
                 alive = hidden[at, half].astype(jnp.float32) > 0.0
                 second[at, half] = jnp.where(alive, whole, 0.0)
     products = nt(patches[...], second[...].astype(jnp.bfloat16))
@@ -227,20 +230,6 @@
     packed[225:256, :] = jnp.zeros((31, 128), jnp.float32)
 
 
-def gradient_kernel(
-    x, t, conv_first, conv_second, gain, head, packed,
-    toeplitz_first, forward, backward, patches, hidden, hidden_stack, second, logits, cotangent, cotangent_stack,
-):
-    expand_first(conv_first, toeplitz_first)
-    expand_second(conv_second, forward, backward)
-    clear_ends(hidden_stack)
-    clear_ends(cotangent_stack)
-    crop_gradients(
-        x, t, gain, head, packed,
-        toeplitz_first, forward, backward, patches, hidden, hidden_stack, second, logits, cotangent, cotangent_stack,
-    )
-
-
 COMPUTE_SCRATCH = [
     pltpu.VMEM((12 * CH, 144), jnp.bfloat16),
     pltpu.VMEM((BAND, 9 * 256), jnp.bfloat16),
@@ -255,31 +244,7 @@
 ]
 
 
-def gradients(x, t, conv_first, conv_second, norm_gain, head_weight):
-    head = head_weight.astype(jnp.bfloat16).astype(jnp.float32)
-    return pl.pallas_call(
-        gradient_kernel,
-        out_shape=jax.ShapeDtypeStruct((256, 128), jnp.float32),
-        in_specs=[pl.BlockSpec(memory_space=pltpu.VMEM)] * 6,
-        out_specs=pl.BlockSpec(memory_space=pltpu.VMEM),
-        scratch_shapes=COMPUTE_SCRATCH,
-        compiler_params=pltpu.CompilerParams(vmem_limit_bytes=40 * 1024 * 1024),
-    )(x, t, conv_first, conv_second, norm_gain.reshape(CH, 1), head.reshape(CH, 1))
-
-
-def unpack(total):
-    second = []
-    for dx in range(3):
-        j = 2 - dx
-        second.append(total[0:216, CH * j : CH * j + CH])
-        second.append(total[72 * j : 72 * j + 72, 96:128])
-    second = jnp.concatenate(second, axis=0).reshape(27, CH, CH)
-    first = jnp.concatenate([total[216:225, CH * dx : CH * dx + CH] for dx in range(3)], axis=0)
-    return first, second, total[216, 96:128], total[217, 96:128]
-
-
 MESH = pl.DeviceIdType.MESH
-ROWS = 16
 
 
 def plane_peer(k):
@@ -290,72 +255,198 @@
     return (x * 32 + z * 4 + y, lax.axis_index("pair")), x * 4 + y
 
 
-def column_peer(k):
+def z_peer(k):
     dp = lax.axis_index("dp")
-    z = lax.rem(lax.rem(dp // 4, 8) + k // 2, 8)
-    core = lax.rem(lax.axis_index("pair") + k % 2, 2)
-    return ((dp // 32) * 32 + z * 4 + lax.rem(dp, 4), core), z * 2 + core
-
-
-def sum_kernel(part, out, first, second, send, recv):
+    z = lax.rem(lax.rem(dp // 4, 8) + k, 8)
+    return ((dp // 32) * 32 + z * 4 + lax.rem(dp, 4), lax.axis_index("pair")), z
+
+
+def core_peer(k):
+    core = lax.rem(lax.axis_index("pair") + k, 2)
+    return (lax.axis_index("dp"), core), core
+
+
+PLANE_STEPS = (10, 6, 9, 11, 14, 2, 5, 7, 8, 13, 15, 1, 3, 4, 12)
+Z_STEPS = (4, 3, 5, 2, 6, 1, 7)
+GROUPS = ((plane_peer, PLANE_STEPS), (z_peer, Z_STEPS), (core_peer, (1,)))
+CHIPS, COLUMN, CORES = GROUPS
+
+
+def rows_at(place, count):
+    return pl.ds(pl.multiple_of(place * count, count), count)
+
+
+def greet():
     barrier = pltpu.get_barrier_semaphore()
-    for k in range(1, 16):
-        pl.semaphore_signal(barrier, inc=1, device_id=plane_peer(k)[0], device_id_type=MESH)
-        pl.semaphore_signal(barrier, inc=1, device_id=column_peer(k)[0], device_id_type=MESH)
-    pl.semaphore_wait(barrier, 30)
-    _, plane_me = plane_peer(0)
-    _, column_me = column_peer(0)
-
-    def rows(place):
-        return pl.ds(pl.multiple_of(place * ROWS, ROWS), ROWS)
-
-    def exchange(stage, peer, source, target):
-        copies = []
-        for k in range(1, 16):
-            device, place = peer(k)
-            copy = pltpu.make_async_remote_copy(
-                src_ref=source(place), dst_ref=target,
-                send_sem=send.at[stage, k], recv_sem=recv.at[stage, k],
-                device_id=device, device_id_type=MESH,
-            )
-            copy.start()
-            copies.append(copy)
-        return copies
-
-    copies = exchange(0, plane_peer, lambda place: part.at[rows(place)], first.at[plane_me])
-    first[plane_me] = part[rows(plane_me)]
+    for peer, steps in GROUPS:
+        for k in steps:
+            pl.semaphore_signal(barrier, inc=1, device_id=peer(k)[0], device_id_type=MESH)
+    return lambda: pl.semaphore_wait(barrier, sum(len(steps) for _, steps in GROUPS))
+
+
+def exchange(stage, group, source, target, send, recv):
+    peer, steps = group
+    copies = []
+    for k in steps:
+        device, place = peer(k)
+        copy = pltpu.make_async_remote_copy(
+            src_ref=source(place), dst_ref=target, send_sem=send.at[stage, k], recv_sem=recv.at[stage, k],
+            device_id=device, device_id_type=MESH,
+        )
+        copy.start()
+        copies.append(copy)
+    return copies
+
+
+def finish(copies):
     for copy in copies:
         copy.wait()
+
+
+def reduce_everywhere(packed, out, halves_in, first, second, send, recv):
+    _, core = core_peer(0)
+    _, place = plane_peer(0)
+    _, z = z_peer(0)
+    copies = exchange(2, CORES, lambda other: packed.at[rows_at(other, 128)], halves_in, send, recv)
+    finish(copies)
+    mine = rows_at(core, 128)
+    packed[mine] = packed[mine] + halves_in[...]
+    part = lambda other: pl.ds(pl.multiple_of(core * 128 + other * 8, 8), 8)
+    copies = exchange(3, CHIPS, lambda other: packed.at[part(other)], first.at[place], send, recv)
+    first[place] = packed[part(place)]
+    finish(copies)
     total = first[0]
     for k in range(1, 16):
         total = total + first[k]
-    second[column_me] = total
-    copies = exchange(1, column_peer, lambda place: second.at[column_me], second.at[column_me])
-    for copy in copies:
-        copy.wait()
+    second[z] = total
+    copies = exchange(4, COLUMN, lambda other: second.at[z], second.at[z], send, recv)
+    finish(copies)
     total = second[0]
-    for k in range(1, 16):
+    for k in range(1, 8):
         total = total + second[k]
-    out[rows(plane_me)] = total
-    copies = exchange(2, plane_peer, lambda place: out.at[rows(plane_me)], out.at[rows(plane_me)])
-    for copy in copies:
-        copy.wait()
-
-
-def sum_everywhere(packed):
+    out[part(place)] = total
+    copies = exchange(5, CHIPS, lambda other: out.at[part(place)], out.at[part(place)], send, recv)
+    finish(copies)
+    copies = exchange(6, CORES, lambda other: out.at[mine], out.at[mine], send, recv)
+    finish(copies)
+
+
+def crop_table(counts, ids, corners):
+    shape = (256, 256)
+    count = counts[...].astype(jnp.float32)
+    before = onehot(iota(shape, 0) < iota(shape, 1))
+    starts = nn(count.astype(jnp.bfloat16), before)
+    number = (iota(shape, 0) + 256 * lax.axis_index("pair")).astype(jnp.float32)
+    total = jnp.zeros((256, 4), jnp.float32)
+    for s in range(MOST):
+        chosen = onehot((number == starts + s) & (count > s))
+        table = jnp.concatenate([ids[s : s + 1, :], corners[s]], axis=0)
+        total = total + nt(chosen, table.astype(jnp.bfloat16))
+    return total
+
+
+def as_number(condition_shape, axis):
+    return iota(condition_shape, axis).astype(jnp.float32)
+
+
+def column(ref):
+    eye = iota((CH, CH), 0) == iota((CH, CH), 1)
+    return jnp.sum(jnp.where(eye, ref[...], 0.0), axis=1, keepdims=True)
+
+
+def step_kernel(
+    pool, counts, ids, corners, conv_first, conv_second, gain_ref, head_ref,
+    out,
+    gathered, arrived, leaving, landed, spots, packed, halves_in, first, second_sums, send, recv,
+    toeplitz_first, forward, backward, patches, hidden, hidden_stack, second, logits, cotangent, cotangent_stack,
+):
+    wait_for_all = greet()
+    _, place = plane_peer(0)
+    _, z = z_peer(0)
+    table = crop_table(counts, ids, corners)
+    gathered[...] = nn(onehot(table[:, 0:1] == as_number((256, 256), 1)), pool[...]).astype(jnp.bfloat16)
+    wait_for_all()
+    copies = exchange(0, CHIPS, lambda other: gathered.at[rows_at(other, 16)], arrived.at[rows_at(place, 16)], send, recv)
+    arrived[rows_at(place, 16)] = gathered[rows_at(place, 16)]
+    expand_first(conv_first, toeplitz_first)
+    expand_second(conv_second, forward, backward)
+    table = table.astype(jnp.bfloat16)
+    row = iota((128, 1), 0)
+    crop = row // 16 * 2 + row % 16 // 8
+    about = nn(onehot(iota((128, 256), 1) == place * 16 + crop), table)
+    x = jnp.floor((about[:, 1:2] - z.astype(jnp.float32) + 7.0) * 0.125) + (row % 8 // 4).astype(jnp.float32)
+    wanted = (x * 4.0 + (row % 4).astype(jnp.float32)) * 16.0 + crop.astype(jnp.float32)
+    chosen = onehot(wanted == as_number((128, 256), 1))
+    finish(copies)
+    leaving[...] = nn(chosen, arrived[...]).astype(jnp.bfloat16)
+    copies = exchange(1, COLUMN, lambda other: leaving.at[rows_at(other, 16)], landed.at[rows_at(z, 16)], send, recv)
+    landed[rows_at(z, 16)] = leaving[rows_at(z, 16)]
+    clear_ends(hidden_stack)
+    clear_ends(cotangent_stack)
+    gain = column(gain_ref)
+    head = column(head_ref).astype(jnp.bfloat16).astype(jnp.float32)
+    row = iota((128, 1), 0)
+    s, p = row % 32 // 16, row % 16
+    about = nn(onehot(iota((128, 256), 1) == place * 16 + z * 2 + s), table)
+    x = about[:, 1:2] + p.astype(jnp.float32)
+    wanted = (x - 8.0 * jnp.floor(x * 0.125)) * 16.0 + (s * 8 + p // 8 * 4 + row // 32).astype(jnp.float32)
+    chosen = onehot((wanted == as_number((128, 128), 1)) & (p < CROP))
+    lane = iota((1, 256), 1)
+    inside = (lane % SIDE < CROP) & (lane // SIDE < CROP)
+    for s in range(2):
+        y = about[16 * s : 16 * s + 1, 2:3] + (lane // SIDE).astype(jnp.float32)
+        spot = y * BLOCK + about[16 * s : 16 * s + 1, 3:4] + (lane % SIDE).astype(jnp.float32)
+        spots[s] = onehot(jnp.where(inside, spot, -1.0) == as_number((1024, 256), 0))
+    finish(copies)
+    planes = nn(chosen, landed[...]).astype(jnp.bfloat16)
+    images, targets = [], []
+    for s in range(2):
+        whole = jnp.concatenate(
+            [
+                jnp.concatenate([planes[32 * q + 16 * s : 32 * q + 16 * s + 16, 256 * c : 256 * c + 256] for q in range(4)], axis=1)
+                for c in range(2)
+            ],
+            axis=0,
+        )
+        window = nn(whole, spots[s])
+        images.append(window[0:16])
+        targets.append(window[16:28])
+    crop_gradients(
+        images, jnp.concatenate(targets, axis=1), gain, head, packed,
+        toeplitz_first, forward, backward, patches, hidden, hidden_stack, second, logits, cotangent, cotangent_stack,
+    )
+    reduce_everywhere(packed, out, halves_in, first, second_sums, send, recv)
+
+
+SCRATCH = [
+    pltpu.VMEM((256, 512), jnp.bfloat16),
+    pltpu.VMEM((256, 512), jnp.bfloat16),
+    pltpu.VMEM((128, 512), jnp.bfloat16),
+    pltpu.VMEM((128, 512), jnp.bfloat16),
+    pltpu.VMEM((2, 1024, 256), jnp.bfloat16),
+    pltpu.VMEM((256, 128), jnp.float32),
+    pltpu.VMEM((128, 128), jnp.float32),
+    pltpu.VMEM((16, 8, 128), jnp.float32),
+    pltpu.VMEM((8, 8, 128), jnp.float32),
+    pltpu.SemaphoreType.DMA((7, 16)),
+    pltpu.SemaphoreType.DMA((7, 16)),
+]
+
+
+def summed_gradients(pool, crop_ids, crop_corners, counts, conv_first, conv_second, norm_gain, head_weight):
     return pl.pallas_call(
-        sum_kernel,
-        out_shape=jax.ShapeDtypeStruct((16 * ROWS, 128), jnp.float32),
-        in_specs=[pl.BlockSpec(memory_space=pltpu.VMEM)],
+        step_kernel,
+        out_shape=jax.ShapeDtypeStruct((256, 128), jnp.float32),
+        in_specs=[pl.BlockSpec(memory_space=pltpu.VMEM)] * 8,
         out_specs=pl.BlockSpec(memory_space=pltpu.VMEM),
-        scratch_shapes=[
-            pltpu.VMEM((16, ROWS, 128), jnp.float32),
-            pltpu.VMEM((16, ROWS, 128), jnp.float32),
-            pltpu.SemaphoreType.DMA((3, 16)),
-            pltpu.SemaphoreType.DMA((3, 16)),
-        ],
-        compiler_params=pltpu.CompilerParams(collective_id=0, has_side_effects=True),
-    )(packed)
+        scratch_shapes=SCRATCH + COMPUTE_SCRATCH,
+        compiler_params=pltpu.CompilerParams(
+            collective_id=0, has_side_effects=True, vmem_limit_bytes=48 * 1024 * 1024
+        ),
+    )(
+        pool.reshape(256, 512), counts.reshape(1, 256), crop_ids.T, crop_corners.transpose(1, 2, 0),
+        conv_first, conv_second, norm_gain.reshape(1, CH), head_weight.reshape(1, CH),
+    )
 
 
 beta_first = 0.9
@@ -400,39 +491,14 @@
 SHARE = 2
 
 
-def crop_order(counts, position):
-    starts = jnp.cumsum(counts, dtype=jnp.int32) - counts
-    rows = jnp.sum((starts[None, :] <= position[:, None]).astype(jnp.int32), axis=1, dtype=jnp.int32) - 1
-    return rows, position - starts[rows]
-
-
 def shards(
     pool, crop_ids, crop_corners, counts, conv_first, conv_second, norm_gain, head_weight,
     momentum_first, momentum_second, momentum_gain, momentum_head,
     variance_first, variance_second, variance_gain, variance_head,
 ):
-    dp_count = lax.axis_size("dp")
-    pair_index = lax.axis_index("pair")
-    batch_size = counts.shape[0] * SHARE
-    position = pair_index * dp_count * SHARE + jnp.arange(dp_count * SHARE, dtype=jnp.int32)
-    rows, slots = crop_order(counts, position)
-    wanted = crop_ids[rows, slots].reshape(dp_count, SHARE)
-    arrived = lax.all_to_all(pool[wanted], "dp", split_axis=0, concat_axis=3, tiled=True)[0]
-    volumes = arrived.reshape(SHARE, 2, BLOCK, BLOCK, BLOCK)
-    mine = lax.dynamic_slice_in_dim(rows, lax.axis_index("dp") * SHARE, SHARE)
-    mine_slots = lax.dynamic_slice_in_dim(slots, lax.axis_index("dp") * SHARE, SHARE)
-    corners = crop_corners[mine, mine_slots]
-    windows = [
-        lax.dynamic_slice(volumes[s], (0, corners[s, 0], corners[s, 1], corners[s, 2]), (2, CROP, CROP, CROP))
-        for s in range(SHARE)
-    ]
-    windows = jnp.pad(jnp.stack(windows), ((0, 0), (0, 0), (0, 4), (0, 4), (0, 4)))
-    windows = windows.transpose(1, 2, 0, 3, 4).reshape(2, SIDE, LANES)
-    targets = jnp.concatenate([windows[1, 0:12:2], windows[1, 1:12:2]]).astype(jnp.float32)
-    packed = gradients(windows[0], targets, conv_first, conv_second, norm_gain, head_weight)
-    total = sum_everywhere(packed)
+    total = summed_gradients(pool, crop_ids, crop_corners, counts, conv_first, conv_second, norm_gain, head_weight)
     return adam(
-        total, batch_size,
+        total, counts.shape[0] * SHARE,
         (momentum_first, momentum_second, momentum_gain, momentum_head),
         (variance_first, variance_second, variance_gain, variance_head),
     )

time: 79.3 us -> 50.6 us (0.64)
  starting transfers between devices: 16.5 us -> 0 us
  Pallas kernels: 34.7 us -> 47.4 us
  between operations: 12.7 us -> 0.75 us
  local copies, waits for them, and re-layouts: 13.9 us -> 2.31 us
  other arithmetic: 0.84 us -> 0 us
    all_to_all x1 -> x0, starting transfers between devices: 16.5 us -> none  [shards(): lax.all_to_all(pool[wanted], 'dp', split_axis=0, concat_axis=3, tiled=True)]
    pallas_call x2 -> x1, Pallas kernels: 32.2 us -> 44.9 us  [summed_gradients(): pl.pallas_call(step_kernel, out_shape=jax.ShapeDtypeStruct((256, 128), jn...]
    gather x4 -> x0, local copies, waits for them, and re-layouts: 6.9 us -> none  [the longest x1 2.47 us: shards(): wanted = crop_ids[rows, slots].reshape(dp_count, SHARE)]
    unnamed x19 -> x17, local copies, waits for them, and re-layouts: 4.3 us -> 2.31 us
    slice x8 -> x0, local copies, waits for them, and re-layouts: 0.94 us -> none  [the longest x1 0.6 us: shards(): corners[s, 2]]
  transfers between devices with their start and end apart: 1 -> 0, of which waited for: 0 -> 0; matrix products, arithmetic and copies ran while one was open for 2% -> 0% of each run, Pallas kernels for 0% -> 0%
where the time goes in v1:
time: 50.6 us; the launch traced here: 50.4 us
  Pallas kernels  47.4 us (94%)
  local copies, waits for them, and re-layouts  2.31 us (5%)
  between operations  0.75 us (1%)
    pallas_call x1, Pallas kernels, summed_gradients(): pl.pallas_call(step_kernel, out_shape=jax.ShapeDtypeStruct((256, 128), jn...  44.9 us
    pallas_call x1, Pallas kernels, adam(): pl.pallas_call(functools.partial(adam_kernel, 1.0 / batch_size), out_shap...  2.46 us
    unnamed x17, local copies, waits for them, and re-layouts  2.31 us

profile of v1, /device:TPU:1, one launch (start us, length us, event | category | flops | bytes accessed | tf_op | source)
XLA Modules:
  0.0 50.4 jit_solution(15303329550269862954)
XLA Ops:
  0.6 0.0 copy-start.1
  0.6 0.0 copy-start.2
  0.7 0.0 copy-start.3
  0.7 0.0 copy-start.4
  0.7 0.0 copy-start.7
  0.7 1.0 %copy.24 = bf16[32,8,2,256]{3,1,2,0:T(8,128)(2,1)S(1)} copy(bf16[32,8,2,256]{3,2,1,0:T(2,128)(2,1)} %bitcast.21) | data formatting | bytes 524288
  1.7 0.0 copy-start.5
  1.7 0.0 copy-start.6
  1.7 0.0 copy-done.1
  1.7 0.0 copy-done.2
  1.8 0.0 copy-done.3
  1.8 0.0 copy-done.4
  1.8 0.0 copy-done.7
  1.8 0.6 %copy-done.5 = s32[256]{0:T(256)S(1)} copy-done((s32[256]{0:T(256)S(1)}, s32[256]{0:T(256)}, u32[]{:S(2)}) %copy-start.5) | copy-done | bytes 1048
  2.4 0.0 copy-done.6
  2.4 44.9 %shard_map.215.total = f32[256,128]{1,0:T(8,128)S(1)} custom-call(bf16[256,512]{1,0:T(8,128)(2,1)S(1)} %bitcast.15, s32[1,256]{1,0:T(1,128)S(1)} %bitcast.18, s32[3,256]{1,0:T(4,128)S(1)} %bitcast.17, s32[3,3,256]{2,1,0:T(4,128)S(1)} %bitcast.16, f32[27,32]{1,0:T(8,128)S(1)} %copy-done.2, f32[27,32,32]{2,1,0:T(8,128)S(1)} %copy-done.1, ...), custom_call_target="tpu_custom_call" | custom-call | tf_op jit(solution)/shard_map/pallas_call | solution.py:437
  47.3 0.0 copy-start
  47.3 0.6 %copy-done = f32[256,128]{1,0:T(8,128)} copy-done((f32[256,128]{1,0:T(8,128)}, f32[256,128]{1,0:T(8,128)S(1)}, u32[]{:S(2)}) %copy-start) | copy-done | bytes 131096
  48.0 2.5 %shard_map.216 = (f32[27,32]{1,0:T(8,128)}, f32[27,32,32]{2,1,0:T(8,128)}, f32[1,32]{1,0:T(1,128)}, f32[1,32]{1,0:T(1,128)}, f32[27,32]{1,0:T(8,128)}, /*index=5...) custom-call(f32[256,128]{1,0:T(8,128)} %copy-done, f32[27,32]{1,0:T(8,128)} %refs_0_.1, f32[27,32,32]{2,1,0:T(8,128)} %refs_1_.1, ...), custom_call_target="tpu_custom_call" | custom-call | tf_op jit(solution)/shard_map/pallas_call | solution.py:482
Async XLA Ops:
  0.6 1.1 %copy-start.1 = (f32[27,32,32]{2,1,0:T(8,128)S(1)}, f32[27,32,32]{2,1,0:T(8,128)}, u32[]{:S(2)}) copy-start(f32[27,32,32]{2,1,0:T(8,128)} %conv_second.1) | copy-start | bytes 331780
  0.6 1.1 %copy-start.2 = (f32[27,32]{1,0:T(8,128)S(1)}, f32[27,32]{1,0:T(8,128)}, u32[]{:S(2)}) copy-start(f32[27,32]{1,0:T(8,128)} %conv_first.1) | copy-start | bytes 10372
  0.7 1.1 %copy-start.3 = (s32[256,3,3]{0,2,1:T(4,128)S(1)}, s32[256,3,3]{0,2,1:T(4,128)}, u32[]{:S(2)}) copy-start(s32[256,3,3]{0,2,1:T(4,128)} %param.18) | copy-start | bytes 27652
  0.7 1.1 %copy-start.4 = (s32[256,3]{0,1:T(4,128)S(1)}, s32[256,3]{0,1:T(4,128)}, u32[]{:S(2)}) copy-start(s32[256,3]{0,1:T(4,128)} %param.17) | copy-start | bytes 9220
  0.7 1.1 %copy-start.7 = (f32[32]{0:T(128)S(1)}, f32[32]{0:T(128)}, u32[]{:S(2)}) copy-start(f32[32]{0:T(128)} %param.23) | copy-start | bytes 388
  1.7 0.7 %copy-start.5 = (s32[256]{0:T(256)S(1)}, s32[256]{0:T(256)}, u32[]{:S(2)}) copy-start(s32[256]{0:T(256)} %param.19) | copy-start | bytes 3076
  1.7 0.7 %copy-start.6 = (f32[32]{0:T(128)S(1)}, f32[32]{0:T(128)}, u32[]{:S(2)}) copy-start(f32[32]{0:T(128)} %param.22) | copy-start | bytes 388
  47.3 0.7 %copy-start = (f32[256,128]{1,0:T(8,128)}, f32[256,128]{1,0:T(8,128)S(1)}, u32[]{:S(2)}) copy-start(f32[256,128]{1,0:T(8,128)S(1)} %shard_map.215.total) | copy-start | bytes 393220

commit v2 on v1

--- a/solution.py
+++ b/solution.py
@@ -261,15 +261,17 @@
     return ((dp // 32) * 32 + z * 4 + lax.rem(dp, 4), lax.axis_index("pair")), z
 
 
-def core_peer(k):
-    core = lax.rem(lax.axis_index("pair") + k, 2)
-    return (lax.axis_index("dp"), core), core
+def column_peer(k):
+    (dp, _), z = z_peer(k // 2)
+    core = lax.rem(lax.axis_index("pair") + k % 2, 2)
+    return (dp, core), z * 2 + core
 
 
 PLANE_STEPS = (10, 6, 9, 11, 14, 2, 5, 7, 8, 13, 15, 1, 3, 4, 12)
 Z_STEPS = (4, 3, 5, 2, 6, 1, 7)
-GROUPS = ((plane_peer, PLANE_STEPS), (z_peer, Z_STEPS), (core_peer, (1,)))
-CHIPS, COLUMN, CORES = GROUPS
+COLUMN_STEPS = (9, 8, 7, 6, 11, 10, 5, 4, 13, 12, 3, 2, 15, 14, 1)
+CHIPS, DEPTH, COLUMN = (plane_peer, PLANE_STEPS), (z_peer, Z_STEPS), (column_peer, COLUMN_STEPS)
+GROUPS = (CHIPS, COLUMN)
 
 
 def rows_at(place, count):
@@ -303,31 +305,23 @@
         copy.wait()
 
 
-def reduce_everywhere(packed, out, halves_in, first, second, send, recv):
-    _, core = core_peer(0)
+def reduce_everywhere(packed, out, first, second, send, recv):
     _, place = plane_peer(0)
-    _, z = z_peer(0)
-    copies = exchange(2, CORES, lambda other: packed.at[rows_at(other, 128)], halves_in, send, recv)
-    finish(copies)
-    mine = rows_at(core, 128)
-    packed[mine] = packed[mine] + halves_in[...]
-    part = lambda other: pl.ds(pl.multiple_of(core * 128 + other * 8, 8), 8)
-    copies = exchange(3, CHIPS, lambda other: packed.at[part(other)], first.at[place], send, recv)
-    first[place] = packed[part(place)]
+    _, column = column_peer(0)
+    copies = exchange(2, CHIPS, lambda other: packed.at[rows_at(other, 16)], first.at[place], send, recv)
+    first[place] = packed[rows_at(place, 16)]
     finish(copies)
     total = first[0]
     for k in range(1, 16):
         total = total + first[k]
-    second[z] = total
-    copies = exchange(4, COLUMN, lambda other: second.at[z], second.at[z], send, recv)
+    second[column] = total
+    copies = exchange(3, COLUMN, lambda other: second.at[column], second.at[column], send, recv)
     finish(copies)
     total = second[0]
-    for k in range(1, 8):
+    for k in range(1, 16):
         total = total + second[k]
-    out[part(place)] = total
-    copies = exchange(5, CHIPS, lambda other: out.at[part(place)], out.at[part(place)], send, recv)
-    finish(copies)
-    copies = exchange(6, CORES, lambda other: out.at[mine], out.at[mine], send, recv)
+    out[rows_at(place, 16)] = total
+    copies = exchange(4, CHIPS, lambda other: out.at[rows_at(place, 16)], out.at[rows_at(place, 16)], send, recv)
     finish(copies)
 
 
@@ -355,19 +349,47 @@
 
 
 def step_kernel(
-    pool, counts, ids, corners, conv_first, conv_second, gain_ref, head_ref,
+    pool_at, counts_at, ids_at, corners_at, conv_first_at, conv_second_at, gain_at, head_at,
     out,
-    gathered, arrived, leaving, landed, spots, packed, halves_in, first, second_sums, send, recv,
+    pool, counts, ids, corners, conv_first, conv_second, gain_ref, head_ref, loaded,
+    gathered, arrived, leaving, landed, spots, packed, first, second_sums, send, recv,
     toeplitz_first, forward, backward, patches, hidden, hidden_stack, second, logits, cotangent, cotangent_stack,
 ):
     wait_for_all = greet()
+    pairs = (
+        (counts_at, counts), (ids_at, ids), (corners_at, corners), (pool_at, pool),
+        (conv_first_at, conv_first), (conv_second_at, conv_second), (gain_at, gain_ref), (head_at, head_ref),
+    )
+    loads = [pltpu.make_async_copy(*pair, loaded.at[k]) for k, pair in enumerate(pairs)]
+    for load in loads:
+        load.start()
     _, place = plane_peer(0)
     _, z = z_peer(0)
+    for load in loads[0:3]:
+        load.wait()
     table = crop_table(counts, ids, corners)
-    gathered[...] = nn(onehot(table[:, 0:1] == as_number((256, 256), 1)), pool[...]).astype(jnp.bfloat16)
+    loads[3].wait()
+    blocks = pool[...].reshape(512, 256)
+    depth = table[:, 3:4].astype(jnp.int32)
+    narrow = onehot(
+        (iota((256, 128), 0) // BLOCK == iota((256, 128), 1) // SIDE)
+        & (iota((256, 128), 0) % BLOCK == iota((256, 128), 1) % SIDE)
+    )
+    for c in range(2):
+        chosen = onehot(2.0 * table[:, 0:1] + c == as_number((256, 512), 1))
+        slab = nn(chosen, blocks)
+        parts = []
+        for part in (slab[:, 0:128], slab[:, 128:256]):
+            for bit in (16, 8, 4, 2, 1):
+                part = jnp.where((depth & bit) != 0, pltpu.roll(part, 128 - bit, 1), part)
+            parts.append(part)
+        cut = jnp.concatenate(parts, axis=1).astype(jnp.bfloat16)
+        gathered[:, 128 * c : 128 * c + 128] = nn(cut, narrow).astype(jnp.bfloat16)
     wait_for_all()
     copies = exchange(0, CHIPS, lambda other: gathered.at[rows_at(other, 16)], arrived.at[rows_at(place, 16)], send, recv)
     arrived[rows_at(place, 16)] = gathered[rows_at(place, 16)]
+    for load in loads[4:]:
+        load.wait()
     expand_first(conv_first, toeplitz_first)
     expand_second(conv_second, forward, backward)
     table = table.astype(jnp.bfloat16)
@@ -379,7 +401,7 @@
     chosen = onehot(wanted == as_number((128, 256), 1))
     finish(copies)
     leaving[...] = nn(chosen, arrived[...]).astype(jnp.bfloat16)
-    copies = exchange(1, COLUMN, lambda other: leaving.at[rows_at(other, 16)], landed.at[rows_at(z, 16)], send, recv)
+    copies = exchange(1, DEPTH, lambda other: leaving.at[rows_at(other, 16)], landed.at[rows_at(z, 16)], send, recv)
     landed[rows_at(z, 16)] = leaving[rows_at(z, 16)]
     clear_ends(hidden_stack)
     clear_ends(cotangent_stack)
@@ -395,15 +417,15 @@
     inside = (lane % SIDE < CROP) & (lane // SIDE < CROP)
     for s in range(2):
         y = about[16 * s : 16 * s + 1, 2:3] + (lane // SIDE).astype(jnp.float32)
-        spot = y * BLOCK + about[16 * s : 16 * s + 1, 3:4] + (lane % SIDE).astype(jnp.float32)
-        spots[s] = onehot(jnp.where(inside, spot, -1.0) == as_number((1024, 256), 0))
+        spot = y * SIDE + (lane % SIDE).astype(jnp.float32)
+        spots[s] = onehot(jnp.where(inside, spot, -1.0) == as_number((512, 256), 0))
     finish(copies)
     planes = nn(chosen, landed[...]).astype(jnp.bfloat16)
     images, targets = [], []
     for s in range(2):
         whole = jnp.concatenate(
             [
-                jnp.concatenate([planes[32 * q + 16 * s : 32 * q + 16 * s + 16, 256 * c : 256 * c + 256] for q in range(4)], axis=1)
+                jnp.concatenate([planes[32 * q + 16 * s : 32 * q + 16 * s + 16, 128 * c : 128 * c + 128] for q in range(4)], axis=1)
                 for c in range(2)
             ],
             axis=0,
@@ -415,21 +437,29 @@
         images, jnp.concatenate(targets, axis=1), gain, head, packed,
         toeplitz_first, forward, backward, patches, hidden, hidden_stack, second, logits, cotangent, cotangent_stack,
     )
-    reduce_everywhere(packed, out, halves_in, first, second_sums, send, recv)
+    reduce_everywhere(packed, out, first, second_sums, send, recv)
 
 
 SCRATCH = [
-    pltpu.VMEM((256, 512), jnp.bfloat16),
-    pltpu.VMEM((256, 512), jnp.bfloat16),
-    pltpu.VMEM((128, 512), jnp.bfloat16),
-    pltpu.VMEM((128, 512), jnp.bfloat16),
-    pltpu.VMEM((2, 1024, 256), jnp.bfloat16),
+    pltpu.VMEM((256, 2, 256), jnp.bfloat16),
+    pltpu.VMEM((1, 256), jnp.int32),
+    pltpu.VMEM((MOST, 256), jnp.int32),
+    pltpu.VMEM((MOST, 3, 256), jnp.int32),
+    pltpu.VMEM((27, CH), jnp.float32),
+    pltpu.VMEM((27, CH, CH), jnp.float32),
+    pltpu.VMEM((1, CH), jnp.float32),
+    pltpu.VMEM((1, CH), jnp.float32),
+    pltpu.SemaphoreType.DMA((8,)),
+    pltpu.VMEM((256, 256), jnp.bfloat16),
+    pltpu.VMEM((256, 256), jnp.bfloat16),
+    pltpu.VMEM((128, 256), jnp.bfloat16),
+    pltpu.VMEM((128, 256), jnp.bfloat16),
+    pltpu.VMEM((2, 512, 256), jnp.bfloat16),
     pltpu.VMEM((256, 128), jnp.float32),
-    pltpu.VMEM((128, 128), jnp.float32),
-    pltpu.VMEM((16, 8, 128), jnp.float32),
-    pltpu.VMEM((8, 8, 128), jnp.float32),
-    pltpu.SemaphoreType.DMA((7, 16)),
-    pltpu.SemaphoreType.DMA((7, 16)),
+    pltpu.VMEM((16, 16, 128), jnp.float32),
+    pltpu.VMEM((16, 16, 128), jnp.float32),
+    pltpu.SemaphoreType.DMA((5, 16)),
+    pltpu.SemaphoreType.DMA((5, 16)),
 ]
 
 
@@ -437,16 +467,19 @@
     return pl.pallas_call(
         step_kernel,
         out_shape=jax.ShapeDtypeStruct((256, 128), jnp.float32),
-        in_specs=[pl.BlockSpec(memory_space=pltpu.VMEM)] * 8,
+        in_specs=[pl.BlockSpec(memory_space=pltpu.HBM)] * 8,
         out_specs=pl.BlockSpec(memory_space=pltpu.VMEM),
         scratch_shapes=SCRATCH + COMPUTE_SCRATCH,
         compiler_params=pltpu.CompilerParams(
-            collective_id=0, has_side_effects=True, vmem_limit_bytes=48 * 1024 * 1024
+            collective_id=0, has_side_effects=True, vmem_limit_bytes=20 * 1024 * 1024
         ),
-    )(
-        pool.reshape(256, 512), counts.reshape(1, 256), crop_ids.T, crop_corners.transpose(1, 2, 0),
-        conv_first, conv_second, norm_gain.reshape(1, CH), head_weight.reshape(1, CH),
-    )
+    )(*[
+        pltpu.with_memory_space_constraint(value, pltpu.HBM)
+        for value in (
+            pool, counts.reshape(1, 256), crop_ids.T, crop_corners.transpose(1, 2, 0),
+            conv_first, conv_second, norm_gain.reshape(1, CH), head_weight.reshape(1, CH),
+        )
+    ])
 
 
 beta_first = 0.9
@@ -479,11 +512,15 @@
 def adam(total, batch_size, moments, variances):
     rows = [value.reshape(1, CH) if value.ndim == 1 else value for value in (*moments, *variances)]
     shapes = [jax.ShapeDtypeStruct(value.shape, jnp.float32) for value in rows[0:4]]
+    rows = [
+        value if value.ndim == 3 else pltpu.with_memory_space_constraint(value, pltpu.HBM) for value in rows
+    ]
     results = pl.pallas_call(
         functools.partial(adam_kernel, 1.0 / batch_size),
         out_shape=shapes + shapes,
         in_specs=[pl.BlockSpec(memory_space=pltpu.VMEM)] * 9,
         out_specs=[pl.BlockSpec(memory_space=pltpu.VMEM)] * 8,
+        compiler_params=pltpu.CompilerParams(vmem_limit_bytes=8 * 1024 * 1024),
     )(total, *rows)
     return tuple(value.reshape(CH) if value.shape == (1, CH) else value for value in results)
 

time: 50.6 us -> 44.3 us (0.88)
  Pallas kernels: 47.4 us -> 43.4 us
  local copies, waits for them, and re-layouts: 2.31 us -> 0.01 us
    pallas_call x1, Pallas kernels: 44.9 us -> 41.4 us  [summed_gradients(): pl.pallas_call(step_kernel, out_shape=jax.ShapeDtypeStruct((256, 128), jn...]
    unnamed x17 -> x4, local copies, waits for them, and re-layouts: 2.31 us -> 0.01 us
where the time goes in v2:
time: 44.3 us; the launch traced here: 44.1 us
  Pallas kernels  43.4 us (98%)
  between operations  0.68 us (2%)
    pallas_call x1, Pallas kernels, summed_gradients(): pl.pallas_call(step_kernel, out_shape=jax.ShapeDtypeStruct((256, 128), jn...  41.4 us
    pallas_call x1, Pallas kernels, adam(): pl.pallas_call(functools.partial(adam_kernel, 1.0 / batch_size), out_shap...  1.97 us

profile of v2, /device:TPU:1, one launch (start us, length us, event | category | flops | bytes accessed | tf_op | source)
XLA Modules:
  0.0 44.1 jit_solution(3034758720856313713)
XLA Ops:
  0.6 0.0 copy-start.1
  0.6 0.0 copy-start
  0.7 41.4 %shard_map.215.total = f32[256,128]{1,0:T(8,128)S(1)} custom-call(bf16[256,2,256]{2,1,0:T(2,128)(2,1)} %pool_at.1, s32[1,256]{1,0:T(1,128)} %bitcast.15, s32[3,256]{1,0:T(4,128)} %bitcast.14, s32[3,3,256]{2,1,0:T(4,128)} %bitcast.13, f32[27,32]{1,0:T(8,128)} %conv_first_at.1, f32[27,32,32]{2,1,0:T(8,128)} %conv_second_at.1, f32[1,32]{1,0:T(1,128)} %bitcast.20, ...), custom_call_target="tpu_custom_call" | custom-call | tf_op jit(solution)/shard_map/pallas_call | solution.py:467
  42.1 0.0 copy-done.1
  42.1 0.0 copy-done
  42.1 2.0 %shard_map.216 = (f32[27,32]{1,0:T(8,128)}, f32[27,32,32]{2,1,0:T(8,128)}, f32[1,32]{1,0:T(1,128)}, f32[1,32]{1,0:T(1,128)}, f32[27,32]{1,0:T(8,128)}, /*index=5...) custom-call(f32[256,128]{1,0:T(8,128)S(1)} %shard_map.215.total, f32[27,32]{1,0:T(8,128)} %refs_0_.1, ...), custom_call_target="tpu_custom_call" | custom-call | tf_op jit(solution)/shard_map/pallas_call | solution.py:518
Async XLA Ops:
  0.6 41.5 %copy-start.1 = (f32[27,32,32]{2,1,0:T(8,128)S(1)}, f32[27,32,32]{2,1,0:T(8,128)}, u32[]{:S(2)}) copy-start(f32[27,32,32]{2,1,0:T(8,128)} %refs_5_.1) | copy-start | bytes 331780
  0.6 41.5 %copy-start = (f32[27,32,32]{2,1,0:T(8,128)S(1)}, f32[27,32,32]{2,1,0:T(8,128)}, u32[]{:S(2)}) copy-start(f32[27,32,32]{2,1,0:T(8,128)} %refs_1_.1) | copy-start | bytes 331780

commit v3 on v2

v3 whole, which is shorter than its diff:
```python
import functools

import jax
import jax.numpy as jnp
from jax import lax
from jax.experimental import pallas as pl
from jax.experimental.pallas import tpu as pltpu
from jax.sharding import PartitionSpec as P

CH = 32
CROP = 12
BLOCK = 32
MOST = 3


SIDE = 16
PLANE = CROP * CROP
PITCH = PLANE + 2 * CROP
PART = 384
LANES = 2 * PART
VOXELS = CROP * CROP * CROP
BAND = 6 * CH
TAPS = 9 * BAND


def iota(shape, axis):
    return lax.broadcasted_iota(jnp.int32, shape, axis)


def nt(a, b):
    return lax.dot_general(a, b, (((1,), (1,)), ((), ())), preferred_element_type=jnp.float32)


def nn(a, b):
    return jnp.dot(a, b, preferred_element_type=jnp.float32)


def onehot(condition):
    return jnp.where(condition, 1.0, 0.0).astype(jnp.bfloat16)


def in_crop():
    lane = iota((1, PART), 1)
    return (lane < 2 * PITCH) & (lane % PITCH < PLANE)


def edges(reach):
    z = iota((1, PART), 1) % PITCH % CROP
    return z < CROP - reach, None, z >= reach


def sources(value, masks):
    value = value.astype(jnp.bfloat16)
    return [value if mask is None else jnp.where(mask, value, jnp.zeros_like(value)) for mask in masks]


def moved(source, dy, dz):
    amount = (-(CROP * dy + dz)) % PART
    return (pltpu.roll(source, amount, 1) if amount else source).astype(jnp.bfloat16)


def by_crop(columns):
    return jnp.where(iota((1, PART), 1) < PITCH, columns[0], columns[1])


def crop_sums(value):
    lane = iota((1, PART), 1)
    value = jnp.where(in_crop(), value, 0.0)
    first = jnp.sum(jnp.where(lane < PITCH, value, 0.0), axis=1, keepdims=True)
    return first, jnp.sum(jnp.where(lane >= PITCH, value, 0.0), axis=1, keepdims=True)


def expand_first(conv_first, toeplitz_first):
    weights = conv_first[...].astype(jnp.bfloat16)
    repeat = onehot(iota((12 * CH, CH), 0) % CH == iota((12 * CH, CH), 1))
    row, column = iota((12 * CH, 144), 0), iota((12 * CH, 144), 1)
    place = row // CH
    step = column % 16 - (2 * (place % 6) + place // 6) + 1
    total = jnp.zeros((12 * CH, 144), jnp.float32)
    for dx in range(3):
        tap = onehot(iota((144, 27), 0) // 16 + 9 * dx == iota((144, 27), 1))
        spread = nn(tap, weights).astype(jnp.bfloat16)
        total = jnp.where(step == dx, nt(repeat, spread), total)
    toeplitz_first[...] = total.astype(jnp.bfloat16)


def expand_second(conv_second, forward, backward):
    eye = onehot(iota((CH, CH), 0) == iota((CH, CH), 1))
    zero = jnp.zeros((CH, 256 - 3 * CH), jnp.float32)
    plain, turned = [], []
    for tap in range(9):
        blocks = [conv_second[9 * dx + tap] for dx in range(3)]
        plain.append(jnp.concatenate([blocks[2], blocks[1], blocks[0], zero], axis=1))
        stacked = jnp.concatenate(blocks, axis=0).astype(jnp.bfloat16)
        turned.append(jnp.concatenate([nt(eye, stacked), zero], axis=1))
    for i in range(6):
        rows = slice(i * CH, i * CH + CH)
        amount = (CH * (i - 1)) % 256
        for strips, matrix in ((plain, backward), (turned, forward)):
            bands = [(pltpu.roll(strip, amount, 1) if amount else strip)[:, 0:BAND] for strip in strips]
            matrix[rows, :] = jnp.concatenate(bands, axis=1).astype(jnp.bfloat16)


def crop_gradients(
    image, target, gain, head, packed,
    toeplitz_first, forward, backward, patches, hidden, hidden_stack, second, logits, cotangent, cotangent_stack,
):
    halves = (slice(0, PART), slice(PART, LANES))
    places = [(parity, i) for parity in range(2) for i in range(6)]
    steps = [(tap // 3 - 1, tap % 3 - 1) for tap in range(9)]
    valid = in_crop()
    image = sources(image, edges(1))
    for tap, (dy, dz) in enumerate(steps):
        patches[tap * 16 : tap * 16 + 16, :] = moved(image[dz + 1], dy, dz)
    masks = edges(2)
    for parity, half in enumerate(halves):
        first_map = nn(toeplitz_first[parity * BAND : parity * BAND + BAND, :], patches[...])
        value = jnp.where(valid, jnp.maximum(first_map, 0.0), 0.0)
        hidden[:, half] = value.astype(jnp.bfloat16)
        value = sources(value, masks)
        for tap, (dy, dz) in enumerate(steps):
            hidden_stack[tap * BAND : tap * BAND + BAND, half] = moved(value[dz + 1], 2 * dy, 2 * dz)
    second[...] = nn(forward[...], hidden_stack[...])
    scale = 1.0 / VOXELS
    total = jnp.zeros((CH, PART), jnp.float32)
    for parity, i in places:
        total = total + second[i * CH : i * CH + CH, halves[parity]]
    center = by_crop([value * scale for value in crop_sums(total)])
    total = jnp.zeros((CH, PART), jnp.float32)
    for parity, i in places:
        away = second[i * CH : i * CH + CH, halves[parity]] - center
        total = total + away * away
    inverse = by_crop([lax.rsqrt(value * scale + 1e-05) for value in crop_sums(total)])
    for parity, i in places:
        rows, half, plane = slice(i * CH, i * CH + CH), halves[parity], 2 * i + parity
        hat = (second[rows, half] - center) * inverse
        second[rows, half] = hat
        joined = (jnp.maximum(hat * gain, 0.0) + hidden[rows, half].astype(jnp.float32)).astype(jnp.bfloat16)
        logits[plane : plane + 1, :] = jnp.sum(joined.astype(jnp.float32) * head, axis=0, keepdims=True)
    slope = 1.0 / (1.0 + jnp.exp(-logits[0:12, :])) - target
    logits[0:12, :] = jnp.where(valid, slope * scale, 0.0)
    sum_plain = jnp.zeros((CH, PART), jnp.float32)
    sum_hat = jnp.zeros((CH, PART), jnp.float32)
    sum_head = jnp.zeros((CH, PART), jnp.float32)
    for parity, i in places:
        rows, half, plane = slice(i * CH, i * CH + CH), halves[parity], 2 * i + parity
        hat = second[rows, half]
        normed = hat * gain
        slope = logits[plane : plane + 1, :]
        joined = (jnp.maximum(normed, 0.0) + hidden[rows, half].astype(jnp.float32)).astype(jnp.bfloat16)
        sum_head = sum_head + joined.astype(jnp.float32) * slope
        passed = jnp.where(normed > 0.0, slope, 0.0)
        sum_plain = sum_plain + passed
        sum_hat = sum_hat + passed * hat
    grad_head = sum(crop_sums(sum_head))
    sums_plain = [head * value for value in crop_sums(sum_plain)]
    sums_hat = [head * value for value in crop_sums(sum_hat)]
    grad_gain = sum(sums_hat)
    mean_plain = by_crop([value * scale for value in sums_plain])
    mean_hat = by_crop([value * scale for value in sums_hat])
    factor = jnp.where(valid, inverse * gain, 0.0)
    for parity, i in places:
        rows, half, plane = slice(i * CH, i * CH + CH), halves[parity], 2 * i + parity
        hat = second[rows, half]
        slope = logits[plane : plane + 1, :]
        passed = jnp.where(hat * gain > 0.0, head * slope, 0.0)
        value = factor * (passed - mean_plain - hat * mean_hat)
        cotangent[rows, half] = value.astype(jnp.bfloat16)
        value = sources(value, masks)
        for tap, (dy, dz) in enumerate(steps):
            place = tap * BAND + i * CH
            cotangent_stack[place : place + CH, half] = moved(value[1 - dz], -2 * dy, -2 * dz)
    cotangent[BAND:256, :] = jnp.zeros((256 - BAND, LANES), jnp.bfloat16)
    turned = cotangent[...].T
    lane = iota((CH, 128), 1)
    for tap in range(9):
        products = nn(hidden_stack[tap * BAND : tap * BAND + BAND, :], turned)
        total = jnp.zeros((CH, 256), jnp.float32)
        for i in range(6):
            band = products[i * CH : i * CH + CH, :]
            amount = (-CH * (i - 1)) % 256
            total = total + (pltpu.roll(band, amount, 1) if amount else band)
        total = total[:, 0:128]
        at = tap * CH
        if at < 216:
            count = min(CH, 216 - at)
            packed[at : at + count, :] = jnp.where(lane < 96, total, 0.0)[0:count]
        if at + CH > 216:
            skip = max(0, 216 - at)
            for j in range(3):
                shifted = pltpu.roll(total, 96 - CH * j, 1)
                shifted = jnp.where(lane >= 96, shifted, 0.0)[skip:CH]
                to = 72 * j + at + skip - 216
                packed[to : to + CH - skip, :] = packed[to : to + CH - skip, :] + shifted
    back = nn(backward[...], cotangent_stack[...])
    for parity, i in places:
        rows, half, plane = slice(i * CH, i * CH + CH), halves[parity], 2 * i + parity
        whole = back[rows, half] + head * logits[plane : plane + 1, :]
        alive = hidden[rows, half].astype(jnp.float32) > 0.0
        second[rows, half] = jnp.where(alive, whole, 0.0)
    lane = iota((9, 128), 1)
    small = jnp.zeros((9, 128), jnp.float32)
    products = jnp.concatenate([nt(patches[...], second[:, half].astype(jnp.bfloat16)) for half in halves], axis=1)
    row, column = iota((144, 2 * BAND), 0), iota((144, 2 * BAND), 1)
    place = column // CH
    step = row % 16 - (2 * (place % 6) + place // 6) + 1
    for dx in range(3):
        part = jnp.where(step == dx, products, 0.0)
        part = jnp.sum(part.reshape(9, 16, 2 * BAND), axis=1)
        part = part[:, 0:128] + part[:, 128:256] + part[:, 256:384]
        part = part + pltpu.roll(part, 64, 1)
        part = part + pltpu.roll(part, 32, 1)
        small = jnp.where(lane // CH == dx, part, small)
    packed[216:225, :] = small
    pick = iota((CH, 128), 0) + 96 == iota((CH, 128), 1)
    packed[216:217, :] = packed[216:217, :] + jnp.sum(jnp.where(pick, grad_gain, 0.0), axis=0, keepdims=True)
    packed[217:218, :] = packed[217:218, :] + jnp.sum(jnp.where(pick, grad_head, 0.0), axis=0, keepdims=True)
    packed[225:256, :] = jnp.zeros((31, 128), jnp.float32)


COMPUTE_SCRATCH = [
    pltpu.VMEM((12 * CH, 144), jnp.bfloat16),
    pltpu.VMEM((BAND, TAPS), jnp.bfloat16),
    pltpu.VMEM((BAND, TAPS), jnp.bfloat16),
    pltpu.VMEM((144, PART), jnp.bfloat16),
    pltpu.VMEM((BAND, LANES), jnp.bfloat16),
    pltpu.VMEM((TAPS, LANES), jnp.bfloat16),
    pltpu.VMEM((BAND, LANES), jnp.float32),
    pltpu.VMEM((16, PART), jnp.float32),
    pltpu.VMEM((256, LANES), jnp.bfloat16),
    pltpu.VMEM((TAPS, LANES), jnp.bfloat16),
]


MESH = pl.DeviceIdType.MESH


def plane_peer(k):
    dp = lax.axis_index("dp")
    x = lax.rem(dp // 32 + k // 4, 4)
    y = lax.rem(lax.rem(dp, 4) + k % 4, 4)
    z = lax.rem(dp // 4, 8)
    return (x * 32 + z * 4 + y, lax.axis_index("pair")), x * 4 + y


def z_peer(k):
    dp = lax.axis_index("dp")
    z = lax.rem(lax.rem(dp // 4, 8) + k, 8)
    return ((dp // 32) * 32 + z * 4 + lax.rem(dp, 4), lax.axis_index("pair")), z


def column_peer(k):
    (dp, _), z = z_peer(k // 2)
    core = lax.rem(lax.axis_index("pair") + k % 2, 2)
    return (dp, core), z * 2 + core


PLANE_STEPS = (10, 6, 9, 11, 14, 2, 5, 7, 8, 13, 15, 1, 3, 4, 12)
Z_STEPS = (4, 3, 5, 2, 6, 1, 7)
COLUMN_STEPS = (9, 8, 7, 6, 11, 10, 5, 4, 13, 12, 3, 2, 15, 14, 1)
CHIPS, DEPTH, COLUMN = (plane_peer, PLANE_STEPS), (z_peer, Z_STEPS), (column_peer, COLUMN_STEPS)
GROUPS = (CHIPS, COLUMN)


def rows_at(place, count):
    return pl.ds(pl.multiple_of(place * count, count), count)


def greet():
    barrier = pltpu.get_barrier_semaphore()
    for peer, steps in GROUPS:
        for k in steps:
            pl.semaphore_signal(barrier, inc=1, device_id=peer(k)[0], device_id_type=MESH)
    return lambda: pl.semaphore_wait(barrier, sum(len(steps) for _, steps in GROUPS))


def exchange(stage, group, source, target, send, recv):
    peer, steps = group
    copies = []
    for k in steps:
        device, place = peer(k)
        copy = pltpu.make_async_remote_copy(
            src_ref=source(place), dst_ref=target, send_sem=send.at[stage, k], recv_sem=recv.at[stage, k],
            device_id=device, device_id_type=MESH,
        )
        copy.start()
        copies.append(copy)
    return copies


def finish(copies):
    for copy in copies:
        copy.wait()


def reduce_everywhere(packed, out, first, second, send, recv):
    _, place = plane_peer(0)
    _, column = column_peer(0)
    copies = exchange(2, CHIPS, lambda other: packed.at[rows_at(other, 16)], first.at[place], send, recv)
    first[place] = packed[rows_at(place, 16)]
    finish(copies)
    total = first[0]
    for k in range(1, 16):
        total = total + first[k]
    second[column] = total
    copies = exchange(3, COLUMN, lambda other: second.at[column], second.at[column], send, recv)
    finish(copies)
    total = second[0]
    for k in range(1, 16):
        total = total + second[k]
    out[rows_at(place, 16)] = total
    copies = exchange(4, CHIPS, lambda other: out.at[rows_at(place, 16)], out.at[rows_at(place, 16)], send, recv)
    finish(copies)


def crop_table(counts, ids, corners):
    shape = (256, 256)
    count = counts[...].astype(jnp.float32)
    before = onehot(iota(shape, 0) < iota(shape, 1))
    starts = nn(count.astype(jnp.bfloat16), before)
    number = (iota(shape, 0) + 256 * lax.axis_index("pair")).astype(jnp.float32)
    total = jnp.zeros((256, 4), jnp.float32)
    for s in range(MOST):
        chosen = onehot((number == starts + s) & (count > s))
        table = jnp.concatenate([ids[s : s + 1, :], corners[s]], axis=0)
        total = total + nt(chosen, table.astype(jnp.bfloat16))
    return total


def as_number(condition_shape, axis):
    return iota(condition_shape, axis).astype(jnp.float32)


def column(ref):
    eye = iota((CH, CH), 0) == iota((CH, CH), 1)
    return jnp.sum(jnp.where(eye, ref[...], 0.0), axis=1, keepdims=True)


def step_kernel(
    pool_at, counts_at, ids_at, corners_at, conv_first_at, conv_second_at, gain_at, head_at, *refs
):
    small_at, moments_at, (out, small, *moments), refs = refs[0:6], refs[6:8], refs[8:12], refs[12:]
    (
    pool, counts, ids, corners, conv_first, conv_second, gain_ref, head_ref, loaded,
    gathered, arrived, leaving, landed, spots, packed, first, second_sums, send, recv,
    toeplitz_first, forward, backward, patches, hidden, hidden_stack, second, logits, cotangent, cotangent_stack,
    ) = refs
    wait_for_all = greet()
    pairs = (
        (counts_at, counts), (ids_at, ids), (corners_at, corners), (pool_at, pool),
        (conv_first_at, conv_first), (conv_second_at, conv_second), (gain_at, gain_ref), (head_at, head_ref),
    ) + tuple((source, small.at[k, 0 : source.shape[0]]) for k, source in enumerate(small_at)) + tuple(zip(moments_at, moments))
    loads = [pltpu.make_async_copy(*pair, loaded.at[k]) for k, pair in enumerate(pairs)]
    for load in loads:
        load.start()
    _, place = plane_peer(0)
    _, z = z_peer(0)
    for load in loads[0:3]:
        load.wait()
    table = crop_table(counts, ids, corners)
    loads[3].wait()
    blocks = pool[...].reshape(512, 256)
    depth = table[:, 3:4].astype(jnp.int32)
    narrow = onehot(
        (iota((256, 128), 0) // BLOCK == iota((256, 128), 1) // SIDE)
        & (iota((256, 128), 0) % BLOCK == iota((256, 128), 1) % SIDE)
    )
    for c in range(2):
        chosen = onehot(2.0 * table[:, 0:1] + c == as_number((256, 512), 1))
        slab = nn(chosen, blocks)
        parts = []
        for part in (slab[:, 0:128], slab[:, 128:256]):
            for bit in (16, 8, 4, 2, 1):
                part = jnp.where((depth & bit) != 0, pltpu.roll(part, 128 - bit, 1), part)
            parts.append(part)
        cut = jnp.concatenate(parts, axis=1).astype(jnp.bfloat16)
        gathered[:, 128 * c : 128 * c + 128] = nn(cut, narrow).astype(jnp.bfloat16)
    wait_for_all()
    copies = exchange(0, CHIPS, lambda other: gathered.at[rows_at(other, 16)], arrived.at[rows_at(place, 16)], send, recv)
    arrived[rows_at(place, 16)] = gathered[rows_at(place, 16)]
    for load in loads[4:]:
        load.wait()
    expand_first(conv_first, toeplitz_first)
    expand_second(conv_second, forward, backward)
    table = table.astype(jnp.bfloat16)
    row = iota((128, 1), 0)
    crop = row // 16 * 2 + row % 16 // 8
    about = nn(onehot(iota((128, 256), 1) == place * 16 + crop), table)
    x = jnp.floor((about[:, 1:2] - z.astype(jnp.float32) + 7.0) * 0.125) + (row % 8 // 4).astype(jnp.float32)
    wanted = (x * 4.0 + (row % 4).astype(jnp.float32)) * 16.0 + crop.astype(jnp.float32)
    chosen = onehot(wanted == as_number((128, 256), 1))
    finish(copies)
    leaving[...] = nn(chosen, arrived[...]).astype(jnp.bfloat16)
    copies = exchange(1, DEPTH, lambda other: leaving.at[rows_at(other, 16)], landed.at[rows_at(z, 16)], send, recv)
    landed[rows_at(z, 16)] = leaving[rows_at(z, 16)]
    gain = column(gain_ref)
    head = column(head_ref).astype(jnp.bfloat16).astype(jnp.float32)
    row = iota((128, 1), 0)
    s, p = row % 32 // 16, row % 16
    about = nn(onehot(iota((128, 256), 1) == place * 16 + z * 2 + s), table)
    x = about[:, 1:2] + p.astype(jnp.float32)
    wanted = (x - 8.0 * jnp.floor(x * 0.125)) * 16.0 + (s * 8 + p // 8 * 4 + row // 32).astype(jnp.float32)
    chosen = onehot((wanted == as_number((128, 128), 1)) & (p < CROP))
    lane = iota((1, PART), 1)
    for s in range(2):
        y = about[16 * s : 16 * s + 1, 2:3] + (lane % PITCH // CROP).astype(jnp.float32)
        spot = y * SIDE + (lane % PITCH % CROP).astype(jnp.float32)
        inside = in_crop() & (lane // PITCH == s)
        spots[s] = onehot(jnp.where(inside, spot, -1.0) == as_number((512, PART), 0))
    finish(copies)
    planes = nn(chosen, landed[...]).astype(jnp.bfloat16)
    window = jnp.zeros((32, PART), jnp.float32)
    for s in range(2):
        whole = jnp.concatenate(
            [
                jnp.concatenate([planes[32 * q + 16 * s : 32 * q + 16 * s + 16, 128 * c : 128 * c + 128] for q in range(4)], axis=1)
                for c in range(2)
            ],
            axis=0,
        )
        window = window + nn(whole, spots[s])
    crop_gradients(
        window[0:16], window[16:28], gain, head, packed,
        toeplitz_first, forward, backward, patches, hidden, hidden_stack, second, logits, cotangent, cotangent_stack,
    )
    reduce_everywhere(packed, out, first, second_sums, send, recv)


SCRATCH = [
    pltpu.VMEM((256, 2, 256), jnp.bfloat16),
    pltpu.VMEM((1, 256), jnp.int32),
    pltpu.VMEM((MOST, 256), jnp.int32),
    pltpu.VMEM((MOST, 3, 256), jnp.int32),
    pltpu.VMEM((27, CH), jnp.float32),
    pltpu.VMEM((27, CH, CH), jnp.float32),
    pltpu.VMEM((1, CH), jnp.float32),
    pltpu.VMEM((1, CH), jnp.float32),
    pltpu.SemaphoreType.DMA((16,)),
    pltpu.VMEM((256, 256), jnp.bfloat16),
    pltpu.VMEM((256, 256), jnp.bfloat16),
    pltpu.VMEM((128, 256), jnp.bfloat16),
    pltpu.VMEM((128, 256), jnp.bfloat16),
    pltpu.VMEM((2, 512, PART), jnp.bfloat16),
    pltpu.VMEM((256, 128), jnp.float32),
    pltpu.VMEM((16, 16, 128), jnp.float32),
    pltpu.VMEM((16, 16, 128), jnp.float32),
    pltpu.SemaphoreType.DMA((5, 16)),
    pltpu.SemaphoreType.DMA((5, 16)),
]


def summed_gradients(pool, crop_ids, crop_corners, counts, conv_first, conv_second, norm_gain, head_weight, small, large):
    return pl.pallas_call(
        step_kernel,
        out_shape=[jax.ShapeDtypeStruct((256, 128), jnp.float32), jax.ShapeDtypeStruct((6, 32, CH), jnp.float32)]
        + [jax.ShapeDtypeStruct((27, CH, CH), jnp.float32)] * 2,
        in_specs=[pl.BlockSpec(memory_space=pltpu.HBM)] * 16,
        out_specs=[pl.BlockSpec(memory_space=pltpu.VMEM)] * 4,
        scratch_shapes=SCRATCH + COMPUTE_SCRATCH,
        compiler_params=pltpu.CompilerParams(
            collective_id=0, has_side_effects=True, vmem_limit_bytes=20 * 1024 * 1024
        ),
    )(*[
        pltpu.with_memory_space_constraint(value, pltpu.HBM)
        for value in (
            pool, counts.reshape(1, 256), crop_ids.T, crop_corners.transpose(1, 2, 0),
            conv_first, conv_second, norm_gain.reshape(1, CH), head_weight.reshape(1, CH),
            *[value.reshape(-1, CH) for value in small],
            *large,
        )
    ])


beta_first = 0.9
beta_second = 0.999


def adam_update(gradient, momentum, variance):
    next_momentum = beta_first * momentum + (1.0 - beta_first) * gradient
    next_variance = beta_second * variance + (1.0 - beta_second) * gradient * gradient
    return next_momentum / (jnp.sqrt(next_variance) + 1e-08), next_momentum


def adam_kernel(inverse_batch, total, small, moment, variance, *refs):
    updates, nexts = refs[0:4], refs[4:8]
    gradient = total[...] * inverse_batch
    for dx in range(3):
        j = 2 - dx
        part = jnp.concatenate(
            [gradient[0:216, CH * j : CH * j + CH], gradient[72 * j : 72 * j + 72, 96:128]], axis=0
        ).reshape(9, CH, CH)
        taps = slice(9 * dx, 9 * dx + 9)
        updates[1][taps], nexts[1][taps] = adam_update(part, moment[taps], variance[taps])
        part = gradient[216:225, CH * dx : CH * dx + CH]
        updates[0][taps], nexts[0][taps] = adam_update(part, small[0, taps], small[3, taps])
    for k in (1, 2):
        part = gradient[215 + k : 216 + k, 96:128]
        updates[k + 1][...], nexts[k + 1][...] = adam_update(part, small[k, 0:1], small[k + 3, 0:1])


def adam(batch_size, total, small, moment, variance):
    shapes = [jax.ShapeDtypeStruct(shape, jnp.float32) for shape in ((27, CH), (27, CH, CH), (1, CH), (1, CH))]
    results = pl.pallas_call(
        functools.partial(adam_kernel, 1.0 / batch_size),
        out_shape=shapes + shapes,
        in_specs=[pl.BlockSpec(memory_space=pltpu.VMEM)] * 4,
        out_specs=[pl.BlockSpec(memory_space=pltpu.VMEM)] * 8,
        compiler_params=pltpu.CompilerParams(vmem_limit_bytes=8 * 1024 * 1024),
    )(total, small, moment, variance)
    return tuple(value.reshape(CH) if value.shape == (1, CH) else value for value in results)


SHARE = 2


def shards(
    pool, crop_ids, crop_corners, counts, conv_first, conv_second, norm_gain, head_weight,
    momentum_first, momentum_second, momentum_gain, momentum_head,
    variance_first, variance_second, variance_gain, variance_head,
):
    moved_on = summed_gradients(
        pool, crop_ids, crop_corners, counts, conv_first, conv_second, norm_gain, head_weight,
        (momentum_first, momentum_gain, momentum_head, variance_first, variance_gain, variance_head),
        (momentum_second, variance_second),
    )
    return adam(counts.shape[0] * SHARE, *moved_on)


def solution(mesh):
    in_specs = (P(None, None, "dp"),) + (P(),) * 15
    return jax.shard_map(shards, mesh=mesh, in_specs=in_specs, out_specs=(P(),) * 8, check_vma=False)
```

time: 44.3 us -> 42.8 us (0.966)
  Pallas kernels: 43.4 us -> 42 us
    pallas_call x1, Pallas kernels: 1.97 us -> 1.2 us  [adam(): pl.pallas_call(functools.partial(adam_kernel, 1.0 / batch_size), out_shap...]
    pallas_call x1, Pallas kernels: 41.4 us -> 40.8 us  [summed_gradients(): pl.pallas_call(step_kernel, out_shape=[jax.ShapeDtypeStruct((256, 128), j...]
where the time goes in v3:
time: 42.8 us; the launch traced here: 42.7 us
  Pallas kernels  42 us (98%)
  between operations  0.65 us (2%)
    pallas_call x1, Pallas kernels, summed_gradients(): pl.pallas_call(step_kernel, out_shape=[jax.ShapeDtypeStruct((256, 128), j...  40.8 us
    pallas_call x1, Pallas kernels, adam(): pl.pallas_call(functools.partial(adam_kernel, 1.0 / batch_size), out_shap...  1.2 us

profile of v3, /device:TPU:1, one launch (start us, length us, event | category | flops | bytes accessed | tf_op | source)
XLA Modules:
  0.0 42.7 jit_solution(996790243838072256)
XLA Ops:
  0.6 40.8 %shard_map.215 = (f32[256,128]{1,0:T(8,128)S(1)}, f32[6,32,32]{2,1,0:T(8,128)S(1)}, f32[27,32,32]{2,1,0:T(8,128)S(1)}, f32[27,32,32]{2,1,0:T(8,128)S(1)}) custom-call(bf16[256,2,256]{2,1,0:T(2,128)(2,1)} %pool_at.1, s32[1,256]{1,0:T(1,128)} %bitcast.15, s32[3,256]{1,0:T(4,128)} %bitcast.14, s32[3,3,256]{2,1,0:T(4,128)} %bitcast.13, f32[27,32]{1,0:T(8,128)} %conv_first_at.1, ...), custom_call_target="tpu_custom_call" | custom-call | tf_op jit(solution)/shard_map/pallas_call | solution.py:453
  41.5 1.2 %shard_map.216 = (f32[27,32]{1,0:T(8,128)}, f32[27,32,32]{2,1,0:T(8,128)}, f32[1,32]{1,0:T(1,128)}, f32[1,32]{1,0:T(1,128)}, f32[27,32]{1,0:T(8,128)}, /*index=5...) custom-call(f32[256,128]{1,0:T(8,128)S(1)} %get-tuple-element.20.total, f32[6,32,32]{2,1,0:T(8,128)S(1)} %get-tuple-element.21.small, ...), custom_call_target="tpu_custom_call" | custom-call | tf_op jit(solution)/shard_map/pallas_call | solution.py:503

commit v4 on v3

--- a/solution.py
+++ b/solution.py
@@ -192,6 +192,17 @@
                 shifted = jnp.where(lane >= 96, shifted, 0.0)[skip:CH]
                 to = 72 * j + at + skip - 216
                 packed[to : to + CH - skip, :] = packed[to : to + CH - skip, :] + shifted
+    return lambda small: first_gradients(
+        small, gain, head, grad_gain, grad_head,
+        backward, patches, hidden, second, logits, cotangent_stack,
+    )
+
+
+def first_gradients(
+    small_sums, gain, head, grad_gain, grad_head, backward, patches, hidden, second, logits, cotangent_stack,
+):
+    halves = (slice(0, PART), slice(PART, LANES))
+    places = [(parity, i) for parity in range(2) for i in range(6)]
     back = nn(backward[...], cotangent_stack[...])
     for parity, i in places:
         rows, half, plane = slice(i * CH, i * CH + CH), halves[parity], 2 * i + parity
@@ -211,11 +222,11 @@
         part = part + pltpu.roll(part, 64, 1)
         part = part + pltpu.roll(part, 32, 1)
         small = jnp.where(lane // CH == dx, part, small)
-    packed[216:225, :] = small
+    small_sums[0:9, :] = small
     pick = iota((CH, 128), 0) + 96 == iota((CH, 128), 1)
-    packed[216:217, :] = packed[216:217, :] + jnp.sum(jnp.where(pick, grad_gain, 0.0), axis=0, keepdims=True)
-    packed[217:218, :] = packed[217:218, :] + jnp.sum(jnp.where(pick, grad_head, 0.0), axis=0, keepdims=True)
-    packed[225:256, :] = jnp.zeros((31, 128), jnp.float32)
+    small_sums[0:1, :] = small_sums[0:1, :] + jnp.sum(jnp.where(pick, grad_gain, 0.0), axis=0, keepdims=True)
+    small_sums[1:2, :] = small_sums[1:2, :] + jnp.sum(jnp.where(pick, grad_head, 0.0), axis=0, keepdims=True)
+    small_sums[9:16, :] = jnp.zeros((7, 128), jnp.float32)
 
 
 COMPUTE_SCRATCH = [
@@ -293,24 +304,33 @@
         copy.wait()
 
 
-def reduce_everywhere(packed, out, first, second, send, recv):
+def added(slots):
+    total = slots[0]
+    for k in range(1, 16):
+        total = total + slots[k]
+    return total
+
+
+def reduce_everywhere(packed, finish_gradients, out, small_out, first, second, small, small_first, small_second, send, recv):
     _, place = plane_peer(0)
     _, column = column_peer(0)
-    copies = exchange(2, CHIPS, lambda other: packed.at[rows_at(other, 16)], first.at[place], send, recv)
+    parts = exchange(2, CHIPS, lambda other: packed.at[rows_at(other, 16)], first.at[place], send, recv)
     first[place] = packed[rows_at(place, 16)]
-    finish(copies)
-    total = first[0]
-    for k in range(1, 16):
-        total = total + first[k]
-    second[column] = total
-    copies = exchange(3, COLUMN, lambda other: second.at[column], second.at[column], send, recv)
-    finish(copies)
-    total = second[0]
-    for k in range(1, 16):
-        total = total + second[k]
-    out[rows_at(place, 16)] = total
-    copies = exchange(4, CHIPS, lambda other: out.at[rows_at(place, 16)], out.at[rows_at(place, 16)], send, recv)
-    finish(copies)
+    finish_gradients(small)
+    smalls = exchange(5, CHIPS, lambda other: small, small_first.at[place], send, recv)
+    small_first[place] = small[...]
+    finish(parts)
+    second[column] = added(first)
+    parts = exchange(3, COLUMN, lambda other: second.at[column], second.at[column], send, recv)
+    finish(smalls)
+    small_second[column] = added(small_first)
+    smalls = exchange(6, COLUMN, lambda other: small_second.at[column], small_second.at[column], send, recv)
+    finish(parts)
+    out[rows_at(place, 16)] = added(second)
+    parts = exchange(4, CHIPS, lambda other: out.at[rows_at(place, 16)], out.at[rows_at(place, 16)], send, recv)
+    finish(smalls)
+    small_out[...] = added(small_second)
+    finish(parts)
 
 
 def crop_table(counts, ids, corners):
@@ -339,10 +359,10 @@
 def step_kernel(
     pool_at, counts_at, ids_at, corners_at, conv_first_at, conv_second_at, gain_at, head_at, *refs
 ):
-    small_at, moments_at, (out, small, *moments), refs = refs[0:6], refs[6:8], refs[8:12], refs[12:]
+    small_at, moments_at, (out, small_out, small, *moments), refs = refs[0:6], refs[6:8], refs[8:13], refs[13:]
     (
     pool, counts, ids, corners, conv_first, conv_second, gain_ref, head_ref, loaded,
-    gathered, arrived, leaving, landed, spots, packed, first, second_sums, send, recv,
+    gathered, arrived, leaving, landed, spots, packed, first, second_sums, small_sums, small_first, small_second, send, recv,
     toeplitz_first, forward, backward, patches, hidden, hidden_stack, second, logits, cotangent, cotangent_stack,
     ) = refs
     wait_for_all = greet()
@@ -419,11 +439,14 @@
             axis=0,
         )
         window = window + nn(whole, spots[s])
-    crop_gradients(
+    packed[216:256, :] = jnp.zeros((40, 128), jnp.float32)
+    finish_gradients = crop_gradients(
         window[0:16], window[16:28], gain, head, packed,
         toeplitz_first, forward, backward, patches, hidden, hidden_stack, second, logits, cotangent, cotangent_stack,
     )
-    reduce_everywhere(packed, out, first, second_sums, send, recv)
+    reduce_everywhere(
+        packed, finish_gradients, out, small_out, first, second_sums, small_sums, small_first, small_second, send, recv
+    )
 
 
 SCRATCH = [
@@ -444,18 +467,21 @@
     pltpu.VMEM((256, 128), jnp.float32),
     pltpu.VMEM((16, 16, 128), jnp.float32),
     pltpu.VMEM((16, 16, 128), jnp.float32),
-    pltpu.SemaphoreType.DMA((5, 16)),
-    pltpu.SemaphoreType.DMA((5, 16)),
+    pltpu.VMEM((16, 128), jnp.float32),
+    pltpu.VMEM((16, 16, 128), jnp.float32),
+    pltpu.VMEM((16, 16, 128), jnp.float32),
+    pltpu.SemaphoreType.DMA((7, 16)),
+    pltpu.SemaphoreType.DMA((7, 16)),
 ]
 
 
 def summed_gradients(pool, crop_ids, crop_corners, counts, conv_first, conv_second, norm_gain, head_weight, small, large):
     return pl.pallas_call(
         step_kernel,
-        out_shape=[jax.ShapeDtypeStruct((256, 128), jnp.float32), jax.ShapeDtypeStruct((6, 32, CH), jnp.float32)]
+        out_shape=[jax.ShapeDtypeStruct(shape, jnp.float32) for shape in ((256, 128), (16, 128), (6, 32, CH))]
         + [jax.ShapeDtypeStruct((27, CH, CH), jnp.float32)] * 2,
         in_specs=[pl.BlockSpec(memory_space=pltpu.HBM)] * 16,
-        out_specs=[pl.BlockSpec(memory_space=pltpu.VMEM)] * 4,
+        out_specs=[pl.BlockSpec(memory_space=pltpu.VMEM)] * 5,
         scratch_shapes=SCRATCH + COMPUTE_SCRATCH,
         compiler_params=pltpu.CompilerParams(
             collective_id=0, has_side_effects=True, vmem_limit_bytes=20 * 1024 * 1024
@@ -481,9 +507,10 @@
     return next_momentum / (jnp.sqrt(next_variance) + 1e-08), next_momentum
 
 
-def adam_kernel(inverse_batch, total, small, moment, variance, *refs):
+def adam_kernel(inverse_batch, total, small_total, small, moment, variance, *refs):
     updates, nexts = refs[0:4], refs[4:8]
     gradient = total[...] * inverse_batch
+    small_gradient = small_total[...] * inverse_batch
     for dx in range(3):
         j = 2 - dx
         part = jnp.concatenate(
@@ -491,22 +518,22 @@
         ).reshape(9, CH, CH)
         taps = slice(9 * dx, 9 * dx + 9)
         updates[1][taps], nexts[1][taps] = adam_update(part, moment[taps], variance[taps])
-        part = gradient[216:225, CH * dx : CH * dx + CH]
+        part = small_gradient[0:9, CH * dx : CH * dx + CH]
         updates[0][taps], nexts[0][taps] = adam_update(part, small[0, taps], small[3, taps])
     for k in (1, 2):
-        part = gradient[215 + k : 216 + k, 96:128]
+        part = small_gradient[k - 1 : k, 96:128]
         updates[k + 1][...], nexts[k + 1][...] = adam_update(part, small[k, 0:1], small[k + 3, 0:1])
 
 
-def adam(batch_size, total, small, moment, variance):
+def adam(batch_size, total, small_total, small, moment, variance):
     shapes = [jax.ShapeDtypeStruct(shape, jnp.float32) for shape in ((27, CH), (27, CH, CH), (1, CH), (1, CH))]
     results = pl.pallas_call(
         functools.partial(adam_kernel, 1.0 / batch_size),
         out_shape=shapes + shapes,
-        in_specs=[pl.BlockSpec(memory_space=pltpu.VMEM)] * 4,
+        in_specs=[pl.BlockSpec(memory_space=pltpu.VMEM)] * 5,
         out_specs=[pl.BlockSpec(memory_space=pltpu.VMEM)] * 8,
         compiler_params=pltpu.CompilerParams(vmem_limit_bytes=8 * 1024 * 1024),
-    )(total, small, moment, variance)
+    )(total, small_total, small, moment, variance)
     return tuple(value.reshape(CH) if value.shape == (1, CH) else value for value in results)
 
 

time: 42.8 us -> 42.3 us (0.988)
    pallas_call x1, Pallas kernels: 40.8 us -> 40.3 us  [summed_gradients(): pl.pallas_call(step_kernel, out_shape=[jax.ShapeDtypeStruct(shape, jnp.fl...]
where the time goes in v4:
time: 42.3 us; the launch traced here: 42.2 us
  Pallas kernels  41.6 us (98%)
  between operations  0.65 us (2%)
    pallas_call x1, Pallas kernels, summed_gradients(): pl.pallas_call(step_kernel, out_shape=[jax.ShapeDtypeStruct(shape, jnp.fl...  40.3 us
    pallas_call x1, Pallas kernels, adam(): pl.pallas_call(functools.partial(adam_kernel, 1.0 / batch_size), out_shap...  1.21 us

profile of v4, /device:TPU:1, one launch (start us, length us, event | category | flops | bytes accessed | tf_op | source)
XLA Modules:
  0.0 42.2 jit_solution(17902607924418091234)
XLA Ops:
  0.6 40.3 %shard_map.215 = (f32[256,128]{1,0:T(8,128)S(1)}, f32[16,128]{1,0:T(8,128)S(1)}, f32[6,32,32]{2,1,0:T(8,128)S(1)}, f32[27,32,32]{2,1,0:T(8,128)S(1)}, f32[27,32,32]{2,1,0:T(8,128)S(1)}) custom-call(bf16[256,2,256]{2,1,0:T(2,128)(2,1)} %pool_at.1, s32[1,256]{1,0:T(1,128)} %bitcast.15, s32[3,256]{1,0:T(4,128)} %bitcast.14, s32[3,3,256]{2,1,0:T(4,128)} %bitcast.13, ...), custom_call_target="tpu_custom_call" | custom-call | tf_op jit(solution)/shard_map/pallas_call | solution.py:479
  41.0 1.2 %shard_map.216 = (f32[27,32]{1,0:T(8,128)}, f32[27,32,32]{2,1,0:T(8,128)}, f32[1,32]{1,0:T(1,128)}, f32[1,32]{1,0:T(1,128)}, f32[27,32]{1,0:T(8,128)}, /*index=5...) custom-call(f32[256,128]{1,0:T(8,128)S(1)} %get-tuple-element.21.total, ...), custom_call_target="tpu_custom_call" | custom-call | tf_op jit(solution)/shard_map/pallas_call | solution.py:530

commit v5 on v3

--- a/solution.py
+++ b/solution.py
@@ -175,12 +175,12 @@
     lane = iota((CH, 128), 1)
     for tap in range(9):
         products = nn(hidden_stack[tap * BAND : tap * BAND + BAND, :], turned)
-        total = jnp.zeros((CH, 256), jnp.float32)
-        for i in range(6):
-            band = products[i * CH : i * CH + CH, :]
-            amount = (-CH * (i - 1)) % 256
-            total = total + (pltpu.roll(band, amount, 1) if amount else band)
-        total = total[:, 0:128]
+        low, high = products[:, 0:128], products[:, 128:256]
+        band = [slice(i * CH, i * CH + CH) for i in range(6)]
+        total = low[band[1]] + high[band[5]] + jnp.where(lane >= CH, pltpu.roll(low[band[0]], CH, 1), 0.0)
+        total = total + pltpu.roll(low[band[2]], 96, 1)
+        for i, amount in ((3, 64), (4, 32)):
+            total = total + pltpu.roll(jnp.where(lane < 128 - amount, high[band[i]], low[band[i]]), amount, 1)
         at = tap * CH
         if at < 216:
             count = min(CH, 216 - at)
@@ -192,6 +192,17 @@
                 shifted = jnp.where(lane >= 96, shifted, 0.0)[skip:CH]
                 to = 72 * j + at + skip - 216
                 packed[to : to + CH - skip, :] = packed[to : to + CH - skip, :] + shifted
+    return lambda small: first_gradients(
+        small, gain, head, grad_gain, grad_head,
+        backward, patches, hidden, second, logits, cotangent_stack,
+    )
+
+
+def first_gradients(
+    small_sums, gain, head, grad_gain, grad_head, backward, patches, hidden, second, logits, cotangent_stack,
+):
+    halves = (slice(0, PART), slice(PART, LANES))
+    places = [(parity, i) for parity in range(2) for i in range(6)]
     back = nn(backward[...], cotangent_stack[...])
     for parity, i in places:
         rows, half, plane = slice(i * CH, i * CH + CH), halves[parity], 2 * i + parity
@@ -211,11 +222,14 @@
         part = part + pltpu.roll(part, 64, 1)
         part = part + pltpu.roll(part, 32, 1)
         small = jnp.where(lane // CH == dx, part, small)
-    packed[216:225, :] = small
     pick = iota((CH, 128), 0) + 96 == iota((CH, 128), 1)
-    packed[216:217, :] = packed[216:217, :] + jnp.sum(jnp.where(pick, grad_gain, 0.0), axis=0, keepdims=True)
-    packed[217:218, :] = packed[217:218, :] + jnp.sum(jnp.where(pick, grad_head, 0.0), axis=0, keepdims=True)
-    packed[225:256, :] = jnp.zeros((31, 128), jnp.float32)
+    small = small + jnp.concatenate(
+        [jnp.sum(jnp.where(pick, value, 0.0), axis=0, keepdims=True) for value in (grad_gain, grad_head)]
+        + [jnp.where(lane[0:1] >= 96, pltpu.roll(small[8:9], 96 - CH * dx, 1), 0.0) for dx in range(3)]
+        + [jnp.zeros((4, 128), jnp.float32)],
+        axis=0,
+    )
+    small_sums[...] = small[0:8]
 
 
 COMPUTE_SCRATCH = [
@@ -293,23 +307,26 @@
         copy.wait()
 
 
-def reduce_everywhere(packed, out, first, second, send, recv):
+def added(slots):
+    total = slots[0].astype(jnp.float32)
+    for k in range(1, 16):
+        total = total + slots[k].astype(jnp.float32)
+    return total
+
+
+def reduce_everywhere(packed, finish_gradients, out, first, second, small, send, recv):
     _, place = plane_peer(0)
     _, column = column_peer(0)
     copies = exchange(2, CHIPS, lambda other: packed.at[rows_at(other, 16)], first.at[place], send, recv)
     first[place] = packed[rows_at(place, 16)]
+    finish_gradients(small)
+    second[column, 16:32] = jnp.concatenate([small[...], jnp.zeros((8, 128), jnp.float32)], axis=0).astype(jnp.bfloat16)
     finish(copies)
-    total = first[0]
-    for k in range(1, 16):
-        total = total + first[k]
-    second[column] = total
+    second[column, 0:16] = added(first).astype(jnp.bfloat16)
     copies = exchange(3, COLUMN, lambda other: second.at[column], second.at[column], send, recv)
     finish(copies)
-    total = second[0]
-    for k in range(1, 16):
-        total = total + second[k]
-    out[rows_at(place, 16)] = total
-    copies = exchange(4, CHIPS, lambda other: out.at[rows_at(place, 16)], out.at[rows_at(place, 16)], send, recv)
+    out[place] = added(second)[0:24]
+    copies = exchange(4, CHIPS, lambda other: out.at[place], out.at[place], send, recv)
     finish(copies)
 
 
@@ -342,7 +359,7 @@
     small_at, moments_at, (out, small, *moments), refs = refs[0:6], refs[6:8], refs[8:12], refs[12:]
     (
     pool, counts, ids, corners, conv_first, conv_second, gain_ref, head_ref, loaded,
-    gathered, arrived, leaving, landed, spots, packed, first, second_sums, send, recv,
+    gathered, arrived, leaving, landed, spots, packed, first, second_sums, small_sums, send, recv,
     toeplitz_first, forward, backward, patches, hidden, hidden_stack, second, logits, cotangent, cotangent_stack,
     ) = refs
     wait_for_all = greet()
@@ -419,11 +436,14 @@
             axis=0,
         )
         window = window + nn(whole, spots[s])
-    crop_gradients(
+    packed[216:256, :] = jnp.zeros((40, 128), jnp.float32)
+    finish_gradients = crop_gradients(
         window[0:16], window[16:28], gain, head, packed,
         toeplitz_first, forward, backward, patches, hidden, hidden_stack, second, logits, cotangent, cotangent_stack,
     )
-    reduce_everywhere(packed, out, first, second_sums, send, recv)
+    reduce_everywhere(
+        packed, finish_gradients, out, first, second_sums, small_sums, send, recv
+    )
 
 
 SCRATCH = [
@@ -443,7 +463,8 @@
     pltpu.VMEM((2, 512, PART), jnp.bfloat16),
     pltpu.VMEM((256, 128), jnp.float32),
     pltpu.VMEM((16, 16, 128), jnp.float32),
-    pltpu.VMEM((16, 16, 128), jnp.float32),
+    pltpu.VMEM((16, 32, 128), jnp.bfloat16),
+    pltpu.VMEM((8, 128), jnp.float32),
     pltpu.SemaphoreType.DMA((5, 16)),
     pltpu.SemaphoreType.DMA((5, 16)),
 ]
@@ -452,7 +473,7 @@
 def summed_gradients(pool, crop_ids, crop_corners, counts, conv_first, conv_second, norm_gain, head_weight, small, large):
     return pl.pallas_call(
         step_kernel,
-        out_shape=[jax.ShapeDtypeStruct((256, 128), jnp.float32), jax.ShapeDtypeStruct((6, 32, CH), jnp.float32)]
+        out_shape=[jax.ShapeDtypeStruct(shape, jnp.float32) for shape in ((16, 24, 128), (6, 32, CH))]
         + [jax.ShapeDtypeStruct((27, CH, CH), jnp.float32)] * 2,
         in_specs=[pl.BlockSpec(memory_space=pltpu.HBM)] * 16,
         out_specs=[pl.BlockSpec(memory_space=pltpu.VMEM)] * 4,
@@ -483,7 +504,8 @@
 
 def adam_kernel(inverse_batch, total, small, moment, variance, *refs):
     updates, nexts = refs[0:4], refs[4:8]
-    gradient = total[...] * inverse_batch
+    gradient = total[:, 0:16].reshape(256, 128) * inverse_batch
+    small_gradient = added(total[:, 16:24]) * inverse_batch
     for dx in range(3):
         j = 2 - dx
         part = jnp.concatenate(
@@ -491,10 +513,10 @@
         ).reshape(9, CH, CH)
         taps = slice(9 * dx, 9 * dx + 9)
         updates[1][taps], nexts[1][taps] = adam_update(part, moment[taps], variance[taps])
-        part = gradient[216:225, CH * dx : CH * dx + CH]
+        part = jnp.concatenate([small_gradient[:, CH * dx : CH * dx + CH], small_gradient[2 + dx : 3 + dx, 96:128]], axis=0)
         updates[0][taps], nexts[0][taps] = adam_update(part, small[0, taps], small[3, taps])
     for k in (1, 2):
-        part = gradient[215 + k : 216 + k, 96:128]
+        part = small_gradient[k - 1 : k, 96:128]
         updates[k + 1][...], nexts[k + 1][...] = adam_update(part, small[k, 0:1], small[k + 3, 0:1])
 
 

time: 42.8 us -> 41.9 us (0.979)
  Pallas kernels: 42 us -> 41.1 us
    pallas_call x1, Pallas kernels: 40.8 us -> 39.9 us  [summed_gradients(): pl.pallas_call(step_kernel, out_shape=[jax.ShapeDtypeStruct(shape, jnp.fl...]
where the time goes in v5:
time: 41.9 us; the launch traced here: 41.8 us
  Pallas kernels  41.1 us (98%)
  between operations  0.65 us (2%)
    pallas_call x1, Pallas kernels, summed_gradients(): pl.pallas_call(step_kernel, out_shape=[jax.ShapeDtypeStruct(shape, jnp.fl...  39.9 us
    pallas_call x1, Pallas kernels, adam(): pl.pallas_call(functools.partial(adam_kernel, 1.0 / batch_size), out_shap...  1.21 us

profile of v5, /device:TPU:1, one launch (start us, length us, event | category | flops | bytes accessed | tf_op | source)
XLA Modules:
  0.0 41.8 jit_solution(970507624900826066)
XLA Ops:
  0.6 39.9 %shard_map.215 = (f32[16,24,128]{2,1,0:T(8,128)S(1)}, f32[6,32,32]{2,1,0:T(8,128)S(1)}, f32[27,32,32]{2,1,0:T(8,128)S(1)}, f32[27,32,32]{2,1,0:T(8,128)S(1)}) custom-call(bf16[256,2,256]{2,1,0:T(2,128)(2,1)} %pool_at.1, s32[1,256]{1,0:T(1,128)} %bitcast.15, s32[3,256]{1,0:T(4,128)} %bitcast.14, s32[3,3,256]{2,1,0:T(4,128)} %bitcast.13, ...), custom_call_target="tpu_custom_call" | custom-call | tf_op jit(solution)/shard_map/pallas_call | solution.py:474
  40.6 1.2 %shard_map.216 = (f32[27,32]{1,0:T(8,128)}, f32[27,32,32]{2,1,0:T(8,128)}, f32[1,32]{1,0:T(1,128)}, f32[1,32]{1,0:T(1,128)}, f32[27,32]{1,0:T(8,128)}, /*index=5...) custom-call(f32[16,24,128]{2,1,0:T(8,128)S(1)} %get-tuple-element.20.total, ...), custom_call_target="tpu_custom_call" | custom-call | tf_op jit(solution)/shard_map/pallas_call | solution.py:525

commit v6 on v5

--- a/solution.py
+++ b/solution.py
@@ -141,18 +141,14 @@
     logits[0:12, :] = jnp.where(valid, slope * scale, 0.0)
     sum_plain = jnp.zeros((CH, PART), jnp.float32)
     sum_hat = jnp.zeros((CH, PART), jnp.float32)
-    sum_head = jnp.zeros((CH, PART), jnp.float32)
     for parity, i in places:
         rows, half, plane = slice(i * CH, i * CH + CH), halves[parity], 2 * i + parity
         hat = second[rows, half]
         normed = hat * gain
         slope = logits[plane : plane + 1, :]
-        joined = (jnp.maximum(normed, 0.0) + hidden[rows, half].astype(jnp.float32)).astype(jnp.bfloat16)
-        sum_head = sum_head + joined.astype(jnp.float32) * slope
         passed = jnp.where(normed > 0.0, slope, 0.0)
         sum_plain = sum_plain + passed
         sum_hat = sum_hat + passed * hat
-    grad_head = sum(crop_sums(sum_head))
     sums_plain = [head * value for value in crop_sums(sum_plain)]
     sums_hat = [head * value for value in crop_sums(sum_hat)]
     grad_gain = sum(sums_hat)
@@ -164,17 +160,14 @@
         hat = second[rows, half]
         slope = logits[plane : plane + 1, :]
         passed = jnp.where(hat * gain > 0.0, head * slope, 0.0)
-        value = factor * (passed - mean_plain - hat * mean_hat)
-        cotangent[rows, half] = value.astype(jnp.bfloat16)
-        value = sources(value, masks)
-        for tap, (dy, dz) in enumerate(steps):
-            place = tap * BAND + i * CH
-            cotangent_stack[place : place + CH, half] = moved(value[1 - dz], -2 * dy, -2 * dz)
+        cotangent[rows, half] = (factor * (passed - mean_plain - hat * mean_hat)).astype(jnp.bfloat16)
     cotangent[BAND:256, :] = jnp.zeros((256 - BAND, LANES), jnp.bfloat16)
     turned = cotangent[...].T
     lane = iota((CH, 128), 1)
     for tap in range(9):
-        products = nn(hidden_stack[tap * BAND : tap * BAND + BAND, :], turned)
+        if tap % 3 == 0:
+            three = nn(hidden_stack[tap * BAND : tap * BAND + 3 * BAND, :], turned)
+        products = three[tap % 3 * BAND : tap % 3 * BAND + BAND]
         low, high = products[:, 0:128], products[:, 128:256]
         band = [slice(i * CH, i * CH + CH) for i in range(6)]
         total = low[band[1]] + high[band[5]] + jnp.where(lane >= CH, pltpu.roll(low[band[0]], CH, 1), 0.0)
@@ -193,22 +186,33 @@
                 to = 72 * j + at + skip - 216
                 packed[to : to + CH - skip, :] = packed[to : to + CH - skip, :] + shifted
     return lambda small: first_gradients(
-        small, gain, head, grad_gain, grad_head,
-        backward, patches, hidden, second, logits, cotangent_stack,
+        small, gain, head, grad_gain, backward, patches, hidden, second, logits, cotangent, cotangent_stack,
     )
 
 
 def first_gradients(
-    small_sums, gain, head, grad_gain, grad_head, backward, patches, hidden, second, logits, cotangent_stack,
+    small_sums, gain, head, grad_gain, backward, patches, hidden, second, logits, cotangent, cotangent_stack,
 ):
     halves = (slice(0, PART), slice(PART, LANES))
     places = [(parity, i) for parity in range(2) for i in range(6)]
+    masks = edges(2)
+    for half in halves:
+        value = sources(cotangent[0:BAND, half], masks)
+        for tap in range(9):
+            dy, dz = tap // 3 - 1, tap % 3 - 1
+            cotangent_stack[tap * BAND : tap * BAND + BAND, half] = moved(value[1 - dz], -2 * dy, -2 * dz)
     back = nn(backward[...], cotangent_stack[...])
+    sum_head = jnp.zeros((CH, PART), jnp.float32)
     for parity, i in places:
         rows, half, plane = slice(i * CH, i * CH + CH), halves[parity], 2 * i + parity
-        whole = back[rows, half] + head * logits[plane : plane + 1, :]
+        slope = logits[plane : plane + 1, :]
+        normed = second[rows, half] * gain
+        joined = (jnp.maximum(normed, 0.0) + hidden[rows, half].astype(jnp.float32)).astype(jnp.bfloat16)
+        sum_head = sum_head + joined.astype(jnp.float32) * slope
+        whole = back[rows, half] + head * slope
         alive = hidden[rows, half].astype(jnp.float32) > 0.0
         second[rows, half] = jnp.where(alive, whole, 0.0)
+    grad_head = sum(crop_sums(sum_head))
     lane = iota((9, 128), 1)
     small = jnp.zeros((9, 128), jnp.float32)
     products = jnp.concatenate([nt(patches[...], second[:, half].astype(jnp.bfloat16)) for half in halves], axis=1)
@@ -273,7 +277,7 @@
 Z_STEPS = (4, 3, 5, 2, 6, 1, 7)
 COLUMN_STEPS = (9, 8, 7, 6, 11, 10, 5, 4, 13, 12, 3, 2, 15, 14, 1)
 CHIPS, DEPTH, COLUMN = (plane_peer, PLANE_STEPS), (z_peer, Z_STEPS), (column_peer, COLUMN_STEPS)
-GROUPS = (CHIPS, COLUMN)
+GROUPS = (COLUMN, CHIPS)
 
 
 def rows_at(place, count):
@@ -314,18 +318,19 @@
     return total
 
 
-def reduce_everywhere(packed, finish_gradients, out, first, second, small, send, recv):
+def reduce_everywhere(packed, finish_gradients, out, leaving, first, second, small, send, recv):
     _, place = plane_peer(0)
     _, column = column_peer(0)
-    copies = exchange(2, CHIPS, lambda other: packed.at[rows_at(other, 16)], first.at[place], send, recv)
-    first[place] = packed[rows_at(place, 16)]
+    leaving[...] = packed[...].astype(jnp.bfloat16)
+    copies = exchange(2, CHIPS, lambda other: leaving.at[rows_at(other, 16)], first.at[place], send, recv)
+    first[place] = leaving[rows_at(place, 16)]
     finish_gradients(small)
     second[column, 16:32] = jnp.concatenate([small[...], jnp.zeros((8, 128), jnp.float32)], axis=0).astype(jnp.bfloat16)
     finish(copies)
     second[column, 0:16] = added(first).astype(jnp.bfloat16)
     copies = exchange(3, COLUMN, lambda other: second.at[column], second.at[column], send, recv)
     finish(copies)
-    out[place] = added(second)[0:24]
+    out[place] = added(second).astype(jnp.bfloat16)
     copies = exchange(4, CHIPS, lambda other: out.at[place], out.at[place], send, recv)
     finish(copies)
 
@@ -359,7 +364,7 @@
     small_at, moments_at, (out, small, *moments), refs = refs[0:6], refs[6:8], refs[8:12], refs[12:]
     (
     pool, counts, ids, corners, conv_first, conv_second, gain_ref, head_ref, loaded,
-    gathered, arrived, leaving, landed, spots, packed, first, second_sums, small_sums, send, recv,
+    gathered, arrived, leaving, landed, spots, packed, summands, first, second_sums, small_sums, send, recv,
     toeplitz_first, forward, backward, patches, hidden, hidden_stack, second, logits, cotangent, cotangent_stack,
     ) = refs
     wait_for_all = greet()
@@ -442,7 +447,7 @@
         toeplitz_first, forward, backward, patches, hidden, hidden_stack, second, logits, cotangent, cotangent_stack,
     )
     reduce_everywhere(
-        packed, finish_gradients, out, first, second_sums, small_sums, send, recv
+        packed, finish_gradients, out, summands, first, second_sums, small_sums, send, recv
     )
 
 
@@ -462,7 +467,8 @@
     pltpu.VMEM((128, 256), jnp.bfloat16),
     pltpu.VMEM((2, 512, PART), jnp.bfloat16),
     pltpu.VMEM((256, 128), jnp.float32),
-    pltpu.VMEM((16, 16, 128), jnp.float32),
+    pltpu.VMEM((256, 128), jnp.bfloat16),
+    pltpu.VMEM((16, 16, 128), jnp.bfloat16),
     pltpu.VMEM((16, 32, 128), jnp.bfloat16),
     pltpu.VMEM((8, 128), jnp.float32),
     pltpu.SemaphoreType.DMA((5, 16)),
@@ -473,7 +479,7 @@
 def summed_gradients(pool, crop_ids, crop_corners, counts, conv_first, conv_second, norm_gain, head_weight, small, large):
     return pl.pallas_call(
         step_kernel,
-        out_shape=[jax.ShapeDtypeStruct(shape, jnp.float32) for shape in ((16, 24, 128), (6, 32, CH))]
+        out_shape=[jax.ShapeDtypeStruct((16, 32, 128), jnp.bfloat16), jax.ShapeDtypeStruct((6, 32, CH), jnp.float32)]
         + [jax.ShapeDtypeStruct((27, CH, CH), jnp.float32)] * 2,
         in_specs=[pl.BlockSpec(memory_space=pltpu.HBM)] * 16,
         out_specs=[pl.BlockSpec(memory_space=pltpu.VMEM)] * 4,
@@ -504,8 +510,8 @@
 
 def adam_kernel(inverse_batch, total, small, moment, variance, *refs):
     updates, nexts = refs[0:4], refs[4:8]
-    gradient = total[:, 0:16].reshape(256, 128) * inverse_batch
-    small_gradient = added(total[:, 16:24]) * inverse_batch
+    gradient = total[:, 0:16].astype(jnp.float32).reshape(256, 128) * inverse_batch
+    small_gradient = added(total[:, 16:32])[0:8] * inverse_batch
     for dx in range(3):
         j = 2 - dx
         part = jnp.concatenate(

time: 41.9 us -> 40.8 us (0.974)
  Pallas kernels: 41.1 us -> 40 us
    pallas_call x1, Pallas kernels: 39.9 us -> 38.8 us  [summed_gradients(): pl.pallas_call(step_kernel, out_shape=[jax.ShapeDtypeStruct((16, 32, 128)...]
where the time goes in v6:
time: 40.8 us; the launch traced here: 40.7 us
  Pallas kernels  40 us (98%)
  between operations  0.65 us (2%)
    pallas_call x1, Pallas kernels, summed_gradients(): pl.pallas_call(step_kernel, out_shape=[jax.ShapeDtypeStruct((16, 32, 128)...  38.8 us
    pallas_call x1, Pallas kernels, adam(): pl.pallas_call(functools.partial(adam_kernel, 1.0 / batch_size), out_shap...  1.21 us

profile of v6, /device:TPU:1, one launch (start us, length us, event | category | flops | bytes accessed | tf_op | source)
XLA Modules:
  0.0 40.7 jit_solution(11977197754036841646)
XLA Ops:
  0.6 38.8 %shard_map.215 = (bf16[16,32,128]{2,1,0:T(8,128)(2,1)S(1)}, f32[6,32,32]{2,1,0:T(8,128)S(1)}, f32[27,32,32]{2,1,0:T(8,128)S(1)}, f32[27,32,32]{2,1,0:T(8,128)S(1)}) custom-call(bf16[256,2,256]{2,1,0:T(2,128)(2,1)} %pool_at.1, s32[1,256]{1,0:T(1,128)} %bitcast.15, s32[3,256]{1,0:T(4,128)} %bitcast.14, s32[3,3,256]{2,1,0:T(4,128)} %bitcast.13, ...), custom_call_target="tpu_custom_call" | custom-call | tf_op jit(solution)/shard_map/pallas_call | solution.py:480
  39.5 1.2 %shard_map.216 = (f32[27,32]{1,0:T(8,128)}, f32[27,32,32]{2,1,0:T(8,128)}, f32[1,32]{1,0:T(1,128)}, f32[1,32]{1,0:T(1,128)}, f32[27,32]{1,0:T(8,128)}, /*index=5...) custom-call(bf16[16,32,128]{2,1,0:T(8,128)(2,1)S(1)} %get-tuple-element.20.total, ...), custom_call_target="tpu_custom_call" | custom-call | tf_op jit(solution)/shard_map/pallas_call | solution.py:531

commit v7 on v6

--- a/solution.py
+++ b/solution.py
@@ -318,6 +318,11 @@
     return total
 
 
+def in_two(value):
+    high = value.astype(jnp.bfloat16)
+    return jnp.concatenate([high, (value - high.astype(jnp.float32)).astype(jnp.bfloat16)], axis=0)
+
+
 def reduce_everywhere(packed, finish_gradients, out, leaving, first, second, small, send, recv):
     _, place = plane_peer(0)
     _, column = column_peer(0)
@@ -325,12 +330,14 @@
     copies = exchange(2, CHIPS, lambda other: leaving.at[rows_at(other, 16)], first.at[place], send, recv)
     first[place] = leaving[rows_at(place, 16)]
     finish_gradients(small)
-    second[column, 16:32] = jnp.concatenate([small[...], jnp.zeros((8, 128), jnp.float32)], axis=0).astype(jnp.bfloat16)
+    second[column, 16:32] = in_two(small[...])
     finish(copies)
     second[column, 0:16] = added(first).astype(jnp.bfloat16)
     copies = exchange(3, COLUMN, lambda other: second.at[column], second.at[column], send, recv)
     finish(copies)
-    out[place] = added(second).astype(jnp.bfloat16)
+    total = added(second)
+    out[place, 0:16] = total[0:16].astype(jnp.bfloat16)
+    out[place, 16:32] = in_two(total[16:24] + total[24:32])
     copies = exchange(4, CHIPS, lambda other: out.at[place], out.at[place], send, recv)
     finish(copies)
 
@@ -511,7 +518,8 @@
 def adam_kernel(inverse_batch, total, small, moment, variance, *refs):
     updates, nexts = refs[0:4], refs[4:8]
     gradient = total[:, 0:16].astype(jnp.float32).reshape(256, 128) * inverse_batch
-    small_gradient = added(total[:, 16:32])[0:8] * inverse_batch
+    small_gradient = added(total[:, 16:32])
+    small_gradient = (small_gradient[0:8] + small_gradient[8:16]) * inverse_batch
     for dx in range(3):
         j = 2 - dx
         part = jnp.concatenate(

time: 40.8 us -> 40.8 us (level)
  no operation moved by 1% of the time
where the time goes in v7:
time: 40.8 us; the launch traced here: 40.7 us
  Pallas kernels  40 us (98%)
  between operations  0.65 us (2%)
    pallas_call x1, Pallas kernels, summed_gradients(): pl.pallas_call(step_kernel, out_shape=[jax.ShapeDtypeStruct((16, 32, 128)...  38.8 us
    pallas_call x1, Pallas kernels, adam(): pl.pallas_call(functools.partial(adam_kernel, 1.0 / batch_size), out_shap...  1.21 us

profile of v7, /device:TPU:1, one launch (start us, length us, event | category | flops | bytes accessed | tf_op | source)
XLA Modules:
  0.0 40.7 jit_solution(17570867079518421035)
XLA Ops:
  0.6 38.8 %shard_map.215 = (bf16[16,32,128]{2,1,0:T(8,128)(2,1)S(1)}, f32[6,32,32]{2,1,0:T(8,128)S(1)}, f32[27,32,32]{2,1,0:T(8,128)S(1)}, f32[27,32,32]{2,1,0:T(8,128)S(1)}) custom-call(bf16[256,2,256]{2,1,0:T(2,128)(2,1)} %pool_at.1, s32[1,256]{1,0:T(1,128)} %bitcast.15, s32[3,256]{1,0:T(4,128)} %bitcast.14, s32[3,3,256]{2,1,0:T(4,128)} %bitcast.13, ...), custom_call_target="tpu_custom_call" | custom-call | tf_op jit(solution)/shard_map/pallas_call | solution.py:487
  39.5 1.2 %shard_map.216 = (f32[27,32]{1,0:T(8,128)}, f32[27,32,32]{2,1,0:T(8,128)}, f32[1,32]{1,0:T(1,128)}, f32[1,32]{1,0:T(1,128)}, f32[27,32]{1,0:T(8,128)}, /*index=5...) custom-call(bf16[16,32,128]{2,1,0:T(8,128)(2,1)S(1)} %get-tuple-element.20.total, ...), custom_call_target="tpu_custom_call" | custom-call | tf_op jit(solution)/shard_map/pallas_call | solution.py:539

commit v8 on v7

--- a/solution.py
+++ b/solution.py
@@ -306,9 +306,10 @@
     return copies
 
 
-def finish(copies):
+def receive(copies, started):
     for copy in copies:
-        copy.wait()
+        copy.wait_recv()
+    started.extend(copies)
 
 
 def added(slots):
@@ -323,7 +324,7 @@
     return jnp.concatenate([high, (value - high.astype(jnp.float32)).astype(jnp.bfloat16)], axis=0)
 
 
-def reduce_everywhere(packed, finish_gradients, out, leaving, first, second, small, send, recv):
+def reduce_everywhere(packed, finish_gradients, out, leaving, first, second, small, send, recv, started):
     _, place = plane_peer(0)
     _, column = column_peer(0)
     leaving[...] = packed[...].astype(jnp.bfloat16)
@@ -331,15 +332,15 @@
     first[place] = leaving[rows_at(place, 16)]
     finish_gradients(small)
     second[column, 16:32] = in_two(small[...])
-    finish(copies)
+    receive(copies, started)
     second[column, 0:16] = added(first).astype(jnp.bfloat16)
     copies = exchange(3, COLUMN, lambda other: second.at[column], second.at[column], send, recv)
-    finish(copies)
+    receive(copies, started)
     total = added(second)
     out[place, 0:16] = total[0:16].astype(jnp.bfloat16)
     out[place, 16:32] = in_two(total[16:24] + total[24:32])
     copies = exchange(4, CHIPS, lambda other: out.at[place], out.at[place], send, recv)
-    finish(copies)
+    receive(copies, started)
 
 
 def crop_table(counts, ids, corners):
@@ -374,13 +375,13 @@
     gathered, arrived, leaving, landed, spots, packed, summands, first, second_sums, small_sums, send, recv,
     toeplitz_first, forward, backward, patches, hidden, hidden_stack, second, logits, cotangent, cotangent_stack,
     ) = refs
-    wait_for_all = greet()
+    wait_for_all, started = greet(), []
     pairs = (
         (counts_at, counts), (ids_at, ids), (corners_at, corners), (pool_at, pool),
         (conv_first_at, conv_first), (conv_second_at, conv_second), (gain_at, gain_ref), (head_at, head_ref),
     ) + tuple((source, small.at[k, 0 : source.shape[0]]) for k, source in enumerate(small_at)) + tuple(zip(moments_at, moments))
     loads = [pltpu.make_async_copy(*pair, loaded.at[k]) for k, pair in enumerate(pairs)]
-    for load in loads:
+    for load in loads[0:4]:
         load.start()
     _, place = plane_peer(0)
     _, z = z_peer(0)
@@ -406,6 +407,8 @@
         gathered[:, 128 * c : 128 * c + 128] = nn(cut, narrow).astype(jnp.bfloat16)
     wait_for_all()
     copies = exchange(0, CHIPS, lambda other: gathered.at[rows_at(other, 16)], arrived.at[rows_at(place, 16)], send, recv)
+    for load in loads[4:]:
+        load.start()
     arrived[rows_at(place, 16)] = gathered[rows_at(place, 16)]
     for load in loads[4:]:
         load.wait()
@@ -418,7 +421,7 @@
     x = jnp.floor((about[:, 1:2] - z.astype(jnp.float32) + 7.0) * 0.125) + (row % 8 // 4).astype(jnp.float32)
     wanted = (x * 4.0 + (row % 4).astype(jnp.float32)) * 16.0 + crop.astype(jnp.float32)
     chosen = onehot(wanted == as_number((128, 256), 1))
-    finish(copies)
+    receive(copies, started)
     leaving[...] = nn(chosen, arrived[...]).astype(jnp.bfloat16)
     copies = exchange(1, DEPTH, lambda other: leaving.at[rows_at(other, 16)], landed.at[rows_at(z, 16)], send, recv)
     landed[rows_at(z, 16)] = leaving[rows_at(z, 16)]
@@ -436,7 +439,7 @@
         spot = y * SIDE + (lane % PITCH % CROP).astype(jnp.float32)
         inside = in_crop() & (lane // PITCH == s)
         spots[s] = onehot(jnp.where(inside, spot, -1.0) == as_number((512, PART), 0))
-    finish(copies)
+    receive(copies, started)
     planes = nn(chosen, landed[...]).astype(jnp.bfloat16)
     window = jnp.zeros((32, PART), jnp.float32)
     for s in range(2):
@@ -454,8 +457,10 @@
         toeplitz_first, forward, backward, patches, hidden, hidden_stack, second, logits, cotangent, cotangent_stack,
     )
     reduce_everywhere(
-        packed, finish_gradients, out, summands, first, second_sums, small_sums, send, recv
+        packed, finish_gradients, out, summands, first, second_sums, small_sums, send, recv, started
     )
+    for copy in started:
+        copy.wait_send()
 
 
 SCRATCH = [

time: 40.8 us -> 40.9 us (level)
  no operation moved by 1% of the time
where the time goes in v8:
time: 40.9 us; the launch traced here: 40.7 us
  Pallas kernels  40.1 us (98%)
  between operations  0.65 us (2%)
    pallas_call x1, Pallas kernels, summed_gradients(): pl.pallas_call(step_kernel, out_shape=[jax.ShapeDtypeStruct((16, 32, 128)...  38.8 us
    pallas_call x1, Pallas kernels, adam(): pl.pallas_call(functools.partial(adam_kernel, 1.0 / batch_size), out_shap...  1.21 us

profile of v8, /device:TPU:1, one launch (start us, length us, event | category | flops | bytes accessed | tf_op | source)
XLA Modules:
  0.0 40.7 jit_solution(7064481474820187724)
XLA Ops:
  0.6 38.8 %shard_map.215 = (bf16[16,32,128]{2,1,0:T(8,128)(2,1)S(1)}, f32[6,32,32]{2,1,0:T(8,128)S(1)}, f32[27,32,32]{2,1,0:T(8,128)S(1)}, f32[27,32,32]{2,1,0:T(8,128)S(1)}) custom-call(bf16[256,2,256]{2,1,0:T(2,128)(2,1)} %pool_at.1, s32[1,256]{1,0:T(1,128)} %bitcast.15, s32[3,256]{1,0:T(4,128)} %bitcast.14, s32[3,3,256]{2,1,0:T(4,128)} %bitcast.13, ...), custom_call_target="tpu_custom_call" | custom-call | tf_op jit(solution)/shard_map/pallas_call | solution.py:492
  39.5 1.2 %shard_map.216 = (f32[27,32]{1,0:T(8,128)}, f32[27,32,32]{2,1,0:T(8,128)}, f32[1,32]{1,0:T(1,128)}, f32[1,32]{1,0:T(1,128)}, f32[27,32]{1,0:T(8,128)}, /*index=5...) custom-call(bf16[16,32,128]{2,1,0:T(8,128)(2,1)S(1)} %get-tuple-element.20.total, ...), custom_call_target="tpu_custom_call" | custom-call | tf_op jit(solution)/shard_map/pallas_call | solution.py:544

commit v9 on v7

--- a/solution.py
+++ b/solution.py
@@ -323,16 +323,39 @@
     return jnp.concatenate([high, (value - high.astype(jnp.float32)).astype(jnp.bfloat16)], axis=0)
 
 
+FILLED = 14
+
+
 def reduce_everywhere(packed, finish_gradients, out, leaving, first, second, small, send, recv):
     _, place = plane_peer(0)
     _, column = column_peer(0)
     leaving[...] = packed[...].astype(jnp.bfloat16)
-    copies = exchange(2, CHIPS, lambda other: leaving.at[rows_at(other, 16)], first.at[place], send, recv)
+    peer, steps = CHIPS
+    copies = []
+    for k in steps:
+        device, other = peer(k)
+        copy = pltpu.make_async_remote_copy(
+            src_ref=leaving.at[rows_at(other, 16)], dst_ref=first.at[place], send_sem=send.at[2, k], recv_sem=recv.at[2, k],
+            device_id=device, device_id_type=MESH,
+        )
+        pl.when(other < FILLED)(copy.start)
+        copies.append((copy, other))
     first[place] = leaving[rows_at(place, 16)]
     finish_gradients(small)
     second[column, 16:32] = in_two(small[...])
-    finish(copies)
-    second[column, 0:16] = added(first).astype(jnp.bfloat16)
+    for copy, other in copies:
+        pl.when(other < FILLED)(copy.wait_send)
+
+    @pl.when(place < FILLED)
+    def _():
+        for copy, _ in copies:
+            copy.wait_recv()
+        second[column, 0:16] = added(first).astype(jnp.bfloat16)
+
+    @pl.when(place >= FILLED)
+    def _():
+        second[column, 0:16] = jnp.zeros((16, 128), jnp.bfloat16)
+
     copies = exchange(3, COLUMN, lambda other: second.at[column], second.at[column], send, recv)
     finish(copies)
     total = added(second)

time: 40.8 us -> 40.7 us (level)
  no operation moved by 1% of the time
where the time goes in v9:
time: 40.7 us; the launch traced here: 40.6 us
  Pallas kernels  39.9 us (98%)
  between operations  0.65 us (2%)
    pallas_call x1, Pallas kernels, summed_gradients(): pl.pallas_call(step_kernel, out_shape=[jax.ShapeDtypeStruct((16, 32, 128)...  38.7 us
    pallas_call x1, Pallas kernels, adam(): pl.pallas_call(functools.partial(adam_kernel, 1.0 / batch_size), out_shap...  1.21 us

profile of v9, /device:TPU:1, one launch (start us, length us, event | category | flops | bytes accessed | tf_op | source)
XLA Modules:
  0.0 40.6 jit_solution(3213791611623368993)
XLA Ops:
  0.6 38.7 %shard_map.215 = (bf16[16,32,128]{2,1,0:T(8,128)(2,1)S(1)}, f32[6,32,32]{2,1,0:T(8,128)S(1)}, f32[27,32,32]{2,1,0:T(8,128)S(1)}, f32[27,32,32]{2,1,0:T(8,128)S(1)}) custom-call(bf16[256,2,256]{2,1,0:T(2,128)(2,1)} %pool_at.1, s32[1,256]{1,0:T(1,128)} %bitcast.15, s32[3,256]{1,0:T(4,128)} %bitcast.14, s32[3,3,256]{2,1,0:T(4,128)} %bitcast.13, ...), custom_call_target="tpu_custom_call" | custom-call | tf_op jit(solution)/shard_map/pallas_call | solution.py:510
  39.4 1.2 %shard_map.216 = (f32[27,32]{1,0:T(8,128)}, f32[27,32,32]{2,1,0:T(8,128)}, f32[1,32]{1,0:T(1,128)}, f32[1,32]{1,0:T(1,128)}, f32[27,32]{1,0:T(8,128)}, /*index=5...) custom-call(bf16[16,32,128]{2,1,0:T(8,128)(2,1)S(1)} %get-tuple-element.20.total, ...), custom_call_target="tpu_custom_call" | custom-call | tf_op jit(solution)/shard_map/pallas_call | solution.py:562
